TPU v7x, 128 devices: a whole 4x4x4 slice. The times are simulated.
128 devices in a mesh: row: 8 (over z_lo, x), col: 16 (over z_hi, y, core).
Axes of the slice: x: 4, y: 4, z: 4 (z_hi: 2, z_lo: 2; z = z_hi * 2 + z_lo), core: 2. Of those that a mesh axis runs over, the one named last changes fastest.
Arguments:
- activations: bfloat16 [32768, 4096], P(('row', 'col')), may hold values from -6 to 6
- out_grads: bfloat16 [32768, 4096], P(('row', 'col')), may hold values from -6 to 6
- proj_act: bfloat16 [4096, 160], replicated, may hold values from -0.09375 to 0.09375
- proj_grad: bfloat16 [4096, 128], replicated, may hold values from -0.09375 to 0.09375
- damping: float32 [20480], replicated, may hold values from 0.3 to 3
Outputs:
- factored: float32 [20480, 20480], P('row', 'col')
All inputs are finite; a program needn't handle non-finite values.
Results may differ from a plain program's by a relative error of at most 0.0003.
Values sent between devices are 32-bit elements; how exact they have to be, the bound alone decides.
No kernel may reach another device: no remote copies, remote signals or barrier semaphores. Data moves between devices by JAX's collectives and lax.ppermute only.
A program may use at most 192 MiB of HBM per device.

v0:
```python
import jax
import jax.numpy as jnp
from jax import lax
from jax.sharding import PartitionSpec as P

SA = 160
SG = 128
TOK_EX = 64
B = 128
PW = 512
PANELS = 2


PRECISE = lax.Precision.HIGHEST


def spread(value, axis, source):
    kept = jnp.where(lax.axis_index(axis) == source, value, 0).astype(value.dtype)
    return lax.psum(kept, axis)


def block_features(length_all, stride, offset):
    positions = jnp.arange(length_all, dtype=jnp.int32)
    return (positions // B * stride + offset) * B + positions % B


def outer_rows(left_rows, right_rows):
    return lax.dot_general(
        left_rows,
        right_rows,
        (((1,), (1,)), ((), ())),
        precision=PRECISE,
        preferred_element_type=jnp.float32,
    )


def inner_cols(left_cols, right_cols):
    return lax.dot_general(
        left_cols,
        right_cols,
        (((0,), (0,)), ((), ())),
        precision=PRECISE,
        preferred_element_type=jnp.float32,
    )


def shards(activations, out_grads, proj_act, proj_grad, damping):
    row_count = lax.axis_size("row")
    col_count = lax.axis_size("col")
    row_index = lax.axis_index("row")
    col_index = lax.axis_index("col")
    act_sketch = jnp.dot(activations, proj_act, preferred_element_type=jnp.float32)
    grad_sketch = jnp.dot(out_grads, proj_grad, preferred_element_type=jnp.float32)
    examples_here = activations.shape[0] // TOK_EX
    sketches = jnp.einsum(
        "eti,etj->eij",
        act_sketch.reshape(examples_here, TOK_EX, SA),
        grad_sketch.reshape(examples_here, TOK_EX, SG),
        precision=PRECISE,
    ) * TOK_EX ** (-0.5)
    features = SA * SG
    sketches = sketches.reshape(examples_here, features)
    rows_here = features // row_count
    cols_here = features // col_count
    example_total = examples_here * row_count * col_count
    by_rows = lax.all_to_all(
        sketches.reshape(examples_here, rows_here // B, row_count, B),
        "row",
        split_axis=2,
        concat_axis=0,
        tiled=True,
    )
    by_rows = by_rows.reshape(row_count * examples_here, rows_here)
    by_cols = lax.all_to_all(
        sketches.reshape(examples_here, cols_here // B, col_count, B),
        "col",
        split_axis=2,
        concat_axis=0,
        tiled=True,
    )
    by_cols = by_cols.reshape(col_count, examples_here, cols_here)
    col_full = lax.all_gather(by_cols, "row", axis=1, tiled=True)
    col_full = col_full.reshape(example_total, cols_here)
    gram_tile = inner_cols(lax.all_gather(by_rows, "col", axis=0, tiled=True), col_full)
    row_feat = block_features(rows_here, row_count, row_index)
    col_feat = block_features(cols_here, col_count, col_index)
    damp_rows = jnp.take(damping, row_feat)
    curv_tile = gram_tile / example_total + jnp.where(
        row_feat[:, None] == col_feat[None, :], damp_rows[:, None], 0.0
    )
    history = []
    blocks_per = PW // B
    for panel_no in range(PANELS):
        first_col = panel_no * PW
        end_col = first_col + PW
        blocks = []
        for piece_no in range(blocks_per):
            global_block = panel_no * blocks_per + piece_no
            holder = global_block % col_count
            local_block = global_block // col_count
            blocks.append(
                spread(curv_tile[:, local_block * B : (local_block + 1) * B], "col", holder)
            )
        columns = jnp.concatenate(blocks, axis=1)
        diag_pieces = []
        for piece_no in range(blocks_per):
            global_block = panel_no * blocks_per + piece_no
            holder = global_block % row_count
            local_block = global_block // row_count
            diag_pieces.append(
                spread(columns[local_block * B : (local_block + 1) * B], "row", holder)
            )
        square = jnp.concatenate(diag_pieces, axis=0)
        factor = jnp.linalg.cholesky(square)
        solved = jax.scipy.linalg.solve_triangular(factor, columns.T, lower=True).T
        solved = jnp.where((row_feat >= first_col)[:, None], solved, 0.0)
        history.append((solved, end_col))
        for piece_no in range(blocks_per):
            global_block = panel_no * blocks_per + piece_no
            holder = global_block % col_count
            local_block = global_block // col_count
            written = jnp.where(
                col_index == holder,
                solved[:, piece_no * B : (piece_no + 1) * B],
                curv_tile[:, local_block * B : (local_block + 1) * B],
            )
            curv_tile = lax.dynamic_update_slice_in_dim(curv_tile, written, local_block * B, 1)
        shared_rows = lax.dynamic_index_in_dim(
            solved.reshape(cols_here // B, col_count // row_count, B, PW),
            col_index // row_count,
            axis=1,
            keepdims=False,
        ).reshape(cols_here, PW)
        partner = spread(shared_rows, "row", col_index % row_count)
        update_mask = (row_feat >= end_col)[:, None] & (col_feat >= end_col)[None, :]
        curv_tile = curv_tile - jnp.where(update_mask, outer_rows(solved, partner), 0.0)
    finished = PANELS * PW
    keep_entry = (col_feat < finished)[None, :] | (row_feat >= finished)[:, None]
    return jnp.where(keep_entry, curv_tile, 0.0)


def solution(mesh):
    placed = (P(("row", "col"), None), P(("row", "col"), None), P(), P(), P())
    return jax.shard_map(
        shards, mesh=mesh, in_specs=placed, out_specs=P("row", "col"), check_vma=False
    )
```

profile of v0, /device:TPU:1, one launch (start us, length us, event | category | flops | bytes accessed | tf_op | source)
XLA Modules:
  0.0 1258.6 jit_solution(17000380048825805809)
XLA Ops:
  12.1 18.2 %all_to_all.30 = f32[4,10,16,128]{3,0,1,2:T(4,128)S(1)} all-to-all(f32[4,10,16,128]{3,0,1,2:T(4,128)S(1)} %copy.35), channel_id=1, replica_groups=mesh['row'=8,'col'=16] {'col'}, dimensions={2} | all-to-all | bytes 655360 | tf_op jit(solution)/shard_map/all_to_all | solution.py:74
  31.5 13.1 %all_to_all.31 = f32[4,20,8,128]{3,0,1,2:T(4,128)S(1)} all-to-all(f32[4,20,8,128]{3,0,1,2:T(4,128)S(1)} %copy.33), channel_id=1, replica_groups=mesh['row'=8,'col'=16] {'row'}, dimensions={2} | all-to-all | bytes 655360 | tf_op jit(solution)/shard_map/all_to_all | solution.py:66
  45.6 13.6 %gather_fusion = f32[2560]{0:T(1024)S(1)} fusion(f32[20480]{0:T(1024)S(1)} %copy-done.2, s32[3072]{0:T(1024)S(1)} %pad_clamp_fusion), kind=kCustom, calls=%fused_computation | custom fusion | bytes 30720 | tf_op jit(solution)/shard_map/jit(_take)/gather | solution.py:87
  59.3 11.2 all-gather.5.cloned.1.call-done
  70.5 4.8 copy.37
  75.2 58.3 %all-gather.3.cloned.1.call-done = f32[512,2560]{1,0:T(8,128)} async-done(((f32[32,2560]{1,0:T(8,128)}), f32[512,2560]{1,0:T(8,128)}) %all-gather.3.cloned.1.call-update) | async-done | bytes 5242896 | tf_op jit(solution)/shard_map/all_gather | solution.py:84
  133.6 26.5 %fusion = f32[2560,1280]{0,1:T(8,128)S(1)} fusion(f32[512,2560]{1,0:T(8,128)} %all-gather.3.cloned.1.call-done, f32[512,1280]{1,0:T(8,128)} %bitcast.165, f32[2560]{0:T(1024)S(1)} %and_select_fusion.2, s32[2560]{0:T(1024)S(1)} %fusion.93, s32[1280]{0:T(1024)S(1)} %fusion.105), kind=kOutput, calls=%fused_computation.8 | convolution fusion | flops 20145766400 | bytes 20997120 | tf_op jit(solution)/shard_map/dot_general | solution.py:38
  160.1 4.9 copy-done.21
  167.7 151.7 %all-reduce.18.cloned.1.call-done = (f32[2560,128]{0,1:T(8,128)}, f32[2560,128]{0,1:T(8,128)}, f32[2560,128]{0,1:T(8,128)}, f32[2560,128]{0,1:T(8,128)}) async-done(((f32[2560,128]{0,1:T(8,128)}, f32[2560,128]{0,1:T(8,128)}, f32[2560,128]{0,1:T(8,128)}, f32[2560,128]{0,1:T(8,128)}), (f32[2560,128]{0,1:T(8,128)}, f32[2560,128]{0,1:T(8,128)}, f32[2560,128]{0,1:T(8,128)}, ...) | async-done | bytes 5242896 | tf_op jit(solution)/shard_map/psum | solution.py:19
  326.6 73.3 %all-reduce.22.cloned.1.call-done = (f32[128,512]{0,1:T(8,128)}, f32[128,512]{0,1:T(8,128)}, f32[128,512]{0,1:T(8,128)}, f32[128,512]{0,1:T(8,128)}) async-done(((f32[128,512]{0,1:T(8,128)}, f32[128,512]{0,1:T(8,128)}, f32[128,512]{0,1:T(8,128)}, f32[128,512]{0,1:T(8,128)}), (f32[128,512]{0,1:T(8,128)}, f32[128,512]{0,1:T(8,128)}, f32[128,512]{0,1:T(8,128)}, ...) | async-done | bytes 1048592 | tf_op jit(solution)/shard_map/psum | solution.py:19
  404.4 11.7 cholesky.286
  416.3 9.8 custom-call.27
  426.7 11.7 cholesky.305
  438.5 10.0 custom-call.28
  449.1 11.7 cholesky.326
  461.5 9.8 custom-call.29
  472.0 11.7 cholesky.343
  488.0 8.0 while.4
  496.0 39.3 %custom-call.30 = f32[4,128,128]{1,2,0:T(8,128)S(1)} custom-call(f32[4,128,128]{2,1,0:T(8,128)S(1)} %get-tuple-element.21), custom_call_target="InvertDiagBlocksLowerTriangular" | custom-call | tf_op jit(solution)/shard_map/jit(_solve_triangular)/triangular_solve | solution.py:115
  541.8 2.9 convolution_subtract_fusion.3
  546.0 4.4 fusion.19
  555.3 7.6 reshape.196
  562.8 12.4 fusion.24
  575.2 5.0 copy.55
  580.3 2.9 constant_dynamic-update-slice_fusion.21
  585.8 3.0 constant_dynamic-update-slice_fusion.20
  591.3 76.3 %all-reduce.12.cloned.1.call-done = f32[1280,512]{0,1:T(8,128)} async-done(((f32[1280,512]{0,1:T(8,128)}), f32[1280,512]{0,1:T(8,128)}) %all-reduce.12.cloned.1.call-update) | async-done | bytes 2621456 | tf_op jit(solution)/shard_map/psum | solution.py:19
  667.7 27.0 %fusion.1 = f32[2560,1280]{0,1:T(8,128)S(1)} fusion(f32[2560,1280]{0,1:T(8,128)} %fusion.39, f32[1280,512]{0,1:T(8,128)} %all-reduce.12.cloned.1.call-done, pred[2560]{0:T(1024)(128)(4,1)S(1)} %broadcast_compare_fusion, pred[1280]{0:T(1024)(128)(4,1)S(1)} %broadcast_compare_fusion.3, f32[128,2560]{1,0:T(8,128)} %copy-done.9, f32[128,2560]{1,0:T(8,128)} %copy-done.5, ...), kind=kOutput, calls=%fused_computation.9 | convolution fusion | flops 20147732480 | bytes 34085120 | tf_op jit(solution)/shard_map/dot_general | solution.py:28
  694.7 4.9 copy-done.22
  702.2 156.7 %all-reduce.16.cloned.1.call-done = (f32[2560,128]{0,1:T(8,128)}, f32[2560,128]{0,1:T(8,128)}, f32[2560,128]{0,1:T(8,128)}, f32[2560,128]{0,1:T(8,128)}) async-done(((f32[2560,128]{0,1:T(8,128)}, f32[2560,128]{0,1:T(8,128)}, f32[2560,128]{0,1:T(8,128)}, f32[2560,128]{0,1:T(8,128)}), (f32[2560,128]{0,1:T(8,128)}, f32[2560,128]{0,1:T(8,128)}, f32[2560,128]{0,1:T(8,128)}, ...) | async-done | bytes 5242896 | tf_op jit(solution)/shard_map/psum | solution.py:19
  866.0 73.4 %all-reduce.20.cloned.1.call-done = (f32[128,512]{0,1:T(8,128)}, f32[128,512]{0,1:T(8,128)}, f32[128,512]{0,1:T(8,128)}, f32[128,512]{0,1:T(8,128)}) async-done(((f32[128,512]{0,1:T(8,128)}, f32[128,512]{0,1:T(8,128)}, f32[128,512]{0,1:T(8,128)}, f32[128,512]{0,1:T(8,128)}), (f32[128,512]{0,1:T(8,128)}, f32[128,512]{0,1:T(8,128)}, f32[128,512]{0,1:T(8,128)}, ...) | async-done | bytes 1048592 | tf_op jit(solution)/shard_map/psum | solution.py:19
  943.9 11.7 cholesky.358
  955.8 9.8 custom-call.31
  966.3 11.7 cholesky.377
  979.5 9.9 custom-call.32
  990.1 11.7 cholesky.398
  1002.5 9.8 custom-call.33
  1013.7 11.7 cholesky.415
  1029.2 8.0 while.5
  1037.2 39.3 %custom-call.34 = f32[4,128,128]{1,2,0:T(8,128)S(1)} custom-call(f32[4,128,128]{2,1,0:T(8,128)S(1)} %get-tuple-element.22), custom_call_target="InvertDiagBlocksLowerTriangular" | custom-call | tf_op jit(solution)/shard_map/jit(_solve_triangular)/triangular_solve | solution.py:115
  1087.1 3.6 fusion.16
  1095.6 7.6 reshape.197
  1103.2 12.4 fusion.25
  1115.6 4.9 copy.54
  1120.5 3.1 constant_dynamic-update-slice_fusion.19
  1128.7 79.2 %all-reduce.14.cloned.1.call-done = f32[1280,512]{0,1:T(8,128)} async-done(((f32[1280,512]{0,1:T(8,128)}), f32[1280,512]{0,1:T(8,128)}) %all-reduce.14.cloned.1.call-update) | async-done | bytes 2621456 | tf_op jit(solution)/shard_map/psum | solution.py:19
  1207.9 29.6 %fusion.3 = f32[2560,1280]{0,1:T(8,128)} fusion(f32[2560,1280]{0,1:T(8,128)} %fusion.36, f32[1280,512]{0,1:T(8,128)} %all-reduce.14.cloned.1.call-done, pred[2560]{0:T(1024)(128)(4,1)S(1)} %broadcast_compare_fusion.1, pred[1280]{0:T(1024)(128)(4,1)S(1)} %get-tuple-element.107, pred[1280]{0:T(1024)(128)(4,1)S(1)} %get-tuple-element.108, ...), kind=kOutput, calls=%fused_computation.11 | convolution fusion | flops 20154286080 | bytes 34086400 | tf_op jit(solution)/shard_map/dot_general | solution.py:28
  1237.5 14.0 %copy.43 = f32[2560,1280]{1,0:T(8,128)} copy(f32[2560,1280]{0,1:T(8,128)} %fusion.3) | data formatting | bytes 26214400 | tf_op jit(solution)/shard_map/jit(_where)/select_n | solution.py:139
  (196 shorter events, 100.3 us)
Async XLA Ops:
  6.5 1.6 copy-start
  6.5 3.8 copy-start.20
  6.5 64.0 %all-gather.5.cloned.1.call-start = ((), (), s32[]{:S(2)}) async-start(), calls=%async_computation.3 | async-start | bytes 2949120 | tf_op jit(solution)/shard_map/all_gather | solution.py:82
  8.1 2.2 copy-start.13
  30.3 15.3 %copy-start.2 = (f32[20480]{0:T(1024)S(1)}, f32[20480]{0:T(1024)}, u32[]{:S(2)}) copy-start(f32[20480]{0:T(1024)} %param.12) | copy-start | bytes 245764
  31.2 102.4 %all-gather.3.cloned.1.call-start = ((), (), s32[]{:S(2)}) async-start(), calls=%async_computation.2 | async-start | bytes 5570560 | tf_op jit(solution)/shard_map/all_gather | solution.py:84
  45.5 273.9 %all-reduce.18.cloned.1.call-start = ((), (), s32[]{:S(2)}) async-start(), calls=%async_computation.7 | async-start | bytes 10485760 | tf_op jit(solution)/shard_map/psum | solution.py:19
  160.1 5.0 copy-start.21
  167.7 232.2 %all-reduce.22.cloned.1.call-start = ((), (), s32[]{:S(2)}) async-start(), calls=%async_computation.9 | async-start | bytes 2097152 | tf_op jit(solution)/shard_map/psum | solution.py:19
  319.4 1.7 copy-start.19
  319.4 2.1 copy-start.18
  321.1 1.4 copy-start.16
  322.6 2.3 copy-start.6
  326.0 341.7 %all-reduce.12.cloned.1.call-start = ((), (), s32[]{:S(2)}) async-start(), calls=%async_computation.4 | async-start | bytes 5242880 | tf_op jit(solution)/shard_map/psum | solution.py:19
  496.0 41.9 %copy-start.11 = (f32[512,512]{1,0:T(8,128)}, f32[512,512]{1,0:T(8,128)S(1)}, u32[]{:S(2)}) copy-start(f32[512,512]{1,0:T(8,128)S(1)} %get-tuple-element.250) | copy-start | bytes 3145732
  546.0 5.7 copy-start.5
  551.6 1.1 copy-start.9
  580.2 278.7 %all-reduce.16.cloned.1.call-start = ((), (), s32[]{:S(2)}) async-start(), calls=%async_computation.6 | async-start | bytes 10485760 | tf_op jit(solution)/shard_map/psum | solution.py:19
  694.7 5.0 copy-start.22
  702.2 237.2 %all-reduce.20.cloned.1.call-start = ((), (), s32[]{:S(2)}) async-start(), calls=%async_computation.8 | async-start | bytes 2097152 | tf_op jit(solution)/shard_map/psum | solution.py:19
  859.0 1.7 copy-start.17
  859.0 2.1 copy-start.15
  860.7 1.4 copy-start.14
  862.2 2.3 copy-start.7
  865.5 342.4 %all-reduce.14.cloned.1.call-start = ((), (), s32[]{:S(2)}) async-start(), calls=%async_computation.5 | async-start | bytes 5242880 | tf_op jit(solution)/shard_map/psum | solution.py:19
  943.9 46.2 %copy-start.12 = (f32[512,512]{1,0:T(8,128)}, f32[512,512]{1,0:T(8,128)S(1)}, u32[]{:S(2)}) copy-start(f32[512,512]{1,0:T(8,128)S(1)} %fusion.42) | copy-start | bytes 3145732
  1001.8 81.4 %slice-start.2 = ((s8[5242880]{0:T(1024)(128)(4,1)}), s8[1048576]{0:T(1024)(128)(4,1)S(1)}, s32[]{:S(2)}) async-start(s8[5242880]{0:T(1024)(128)(4,1)} %bitcast.159), calls=%async_computation.12 | async-start | bytes 2097152
  1037.2 39.3 %copy-start.10 = (f32[512,512]{1,0:T(8,128)}, f32[512,512]{1,0:T(8,128)S(1)}, u32[]{:S(2)}) copy-start(f32[512,512]{1,0:T(8,128)S(1)} %get-tuple-element.249) | copy-start | bytes 3145732
  1076.6 6.6 slice-start.3
  1083.2 8.8 copy-start.3
  1087.0 4.9 copy-start.4
  1092.0 1.1 copy-start.8
  1120.5 5.7 slice-start
  1120.5 5.7 slice-start.1
  1237.5 14.1 %copy-start.1 = (bf16[256,4096]{1,0:T(8,128)(2,1)S(1)}, bf16[256,4096]{1,0:T(8,128)(2,1)}, u32[]{:S(2)}) copy-start(bf16[256,4096]{1,0:T(8,128)(2,1)} %param.8) | copy-start | bytes 6291460
Sparse Core Ops, SparseCore 0:
  31.3 39.1 all-gather.4
  72.9 60.6 all-gather.2
  167.8 151.5 all-reduce.17
  326.1 73.7 all-reduce.21
  580.3 87.2 all-reduce.11
  702.3 156.6 all-reduce.15
  865.7 73.7 all-reduce.19
  1120.6 87.2 all-reduce.13
where the time goes:
time: 1270 us; the launch traced here: 1260 us
  waiting for transfers between devices  680 us (54%)
  other arithmetic  294 us (23%)
  matrix products  123 us (10%)
  local copies, waits for them, and re-layouts  109 us (9%)
  blocking collectives  31.4 us (2%)
  between operations  20.1 us (2%)
    psum x6, waiting for transfers between devices, spread(): return lax.psum(kept, axis)  611 us
    another operation x29, other arithmetic, shards(): factor = jnp.linalg.cholesky(square)  158 us
    another operation x5, other arithmetic, shards(): solved = jax.scipy.linalg.solve_triangular(factor, columns.T, lower=True).T  78.9 us
    all_gather x1, waiting for transfers between devices, shards(): lax.all_gather(by_rows, 'col', axis=0, tiled=True)  58.3 us
    dot_general x2, matrix products, outer_rows(): lax.dot_general(left_rows, right_rows, (((1,), (1,)), ((), ())), precisio...  56.6 us
    unnamed x69, local copies, waits for them, and re-layouts  41 us
    select_n x6, other arithmetic, spread(): jnp.where(lax.axis_index(axis) == source, value, 0).astype(value.dtype)  31.9 us
    another operation x14, matrix products, shards(): solved = jax.scipy.linalg.solve_triangular(factor, columns.T, lower=True).T  31.5 us
  transfers between devices with their start and end apart: 8, of which 8 were waited for; matrix products, arithmetic and copies ran while one was open for 3% of the time, Pallas kernels for 0%

commit v1 on v0

v1 whole, which is shorter than its diff:
```python
import functools

import jax
import jax.numpy as jnp
from jax import lax
from jax.experimental import pallas as pl
from jax.experimental.pallas import tpu as pltpu
from jax.sharding import PartitionSpec as P

SA = 160
SG = 128
TOK_EX = 64
B = 128
PW = 512
PANELS = 2
NEX = 512
F = SA * SG
N_ROW = 8
N_COL = 16
FINISHED = PW * PANELS
PANEL_BLOCKS = FINISHED // B

PRECISE = lax.Precision.HIGHEST


def contract(left, right, left_dim, right_dim):
    return lax.dot_general(
        left,
        right,
        (((left_dim,), (right_dim,)), ((), ())),
        precision=PRECISE,
        preferred_element_type=jnp.float32,
    )


def single(left, right):
    return jnp.dot(left, right, preferred_element_type=jnp.float32)


def halves(value):
    high = value.astype(jnp.bfloat16)
    return high, (value - high.astype(jnp.float32)).astype(jnp.bfloat16)


def eliminate(square):
    sub = lax.broadcasted_iota(jnp.int32, (8, B), 0)
    lane = lax.broadcasted_iota(jnp.int32, (8, B), 1)
    tiles = [square[8 * t : 8 * t + 8, :] for t in range(B // 8)]
    for group in range(B // 8):
        first = 8 * group
        cols = {}
        for t in range(group, B // 8):
            for w in range(8):
                cols[t, w] = jnp.broadcast_to(tiles[t][:, first + w : first + w + 1], (8, B))
        scale = None
        for w in range(8):
            here = lane == first + w
            pivot = jnp.broadcast_to(cols[group, w][w : w + 1, :], (8, B))
            later = [jnp.broadcast_to(cols[group, v][w : w + 1, :], (8, B)) for v in range(w + 1, 8)]
            inverse = 1.0 / pivot
            row = jnp.where(here, 1.0, jnp.broadcast_to(tiles[group][w : w + 1, :], (8, B)))
            for t in range(group, B // 8):
                column = cols[t, w]
                cleared = here
                if t == group:
                    column = jnp.where(sub > w, column, 0.0)
                    cleared = here & (sub > w)
                ratio = column * inverse
                for v in range(w + 1, 8):
                    cols[t, v] = cols[t, v] - ratio * later[v - w - 1]
                tiles[t] = jnp.where(cleared, 0.0, tiles[t]) - ratio * row
            root = lax.rsqrt(pivot)
            scale = root if scale is None else jnp.where(sub >= w, root, scale)
        tiles[group] = jnp.where(lane == sub + first, scale, tiles[group] * scale)
    lower = [jnp.where(lane <= sub + 8 * t, tile, 0.0) for t, tile in enumerate(tiles)]
    upper = [
        jnp.where(lane > sub + 8 * t, tile, jnp.where(lane == sub + 8 * t, 1.0 / tile, 0.0))
        for t, tile in enumerate(tiles)
    ]
    return jnp.concatenate(upper, 0), jnp.concatenate(lower, 0)


def chain_kernel(count, x_ref, xt_ref, damp_ref, start_ref, m_ref, y_ref, u_ref, s_ref, last_ref):
    down = lax.broadcasted_iota(jnp.int32, (B, B), 0)
    along = lax.broadcasted_iota(jnp.int32, (B, B), 1)

    def ridge(k):
        return jnp.where(down == along, jnp.broadcast_to(damp_ref[pl.ds(k, 1), :], (B, B)), 0.0)

    m_ref[...] = start_ref[...]
    last_ref[...] = jnp.zeros_like(last_ref)
    first = contract(start_ref[...], x_ref[:, :B], 1, 0)
    s_ref[...] = contract(xt_ref[:B, :], first, 1, 0) + ridge(0)

    def body(k, carry):
        here = pl.multiple_of(k * B, B)
        following = jnp.minimum(k + 1, count - 1)
        there = pl.multiple_of(following * B, B)
        square = s_ref[...]
        last = last_ref[...]
        m_now = m_ref[...] - contract(last, last, 1, 1)
        m_ref[...] = m_now
        pair = jnp.concatenate([x_ref[:, pl.ds(here, B)], x_ref[:, pl.ds(there, B)]], 1)
        both = contract(m_now, pair, 1, 0)
        ahead = contract(xt_ref[pl.ds(there, B), :], both, 1, 0)
        upper, inverse = eliminate(square)
        below = contract(ahead[:, :B], inverse, 1, 1)
        s_ref[...] = ahead[:, B:] - contract(below, below, 1, 1) + ridge(following)
        y_now = contract(both[:, :B], inverse, 1, 1)
        last_ref[...] = y_now
        y_ref[:, pl.ds(here, B)] = y_now
        u_ref[pl.ds(here, B), :] = upper
        return carry

    lax.fori_loop(0, count, body, 0)
    last = last_ref[...]
    m_ref[...] = m_ref[...] - contract(last, last, 1, 1)


def chain(x, xt, damp, start):
    count = x.shape[1] // B
    return pl.pallas_call(
        functools.partial(chain_kernel, count),
        out_shape=(
            jax.ShapeDtypeStruct((NEX, NEX), jnp.float32),
            jax.ShapeDtypeStruct((NEX, count * B), jnp.float32),
            jax.ShapeDtypeStruct((count * B, B), jnp.float32),
        ),
        scratch_shapes=[pltpu.VMEM((B, B), jnp.float32), pltpu.VMEM((NEX, B), jnp.float32)],
        compiler_params=pltpu.CompilerParams(vmem_limit_bytes=24 << 20),
        cost_estimate=pl.CostEstimate(flops=20_000_000_000, bytes_accessed=120_000_000, transcendentals=0),
        name="chain",
    )(x, xt, damp, start)


def tile_kernel(
    place_ref, xr_ref, xc_ref, m_ref, y_ref, u_ref, damp_ref, mid_col, mid_row, row_col, col_row, out_ref, high_ref, low_ref
):
    step = pl.program_id(0)
    row_index = place_ref[0]
    col_index = place_ref[1]
    cols_here = xc_ref.shape[1]
    has_panel = col_index < PANEL_BLOCKS

    @pl.when(step == 0)
    def _():
        to_rows = jnp.where(row_col[...] == mid_row[...], 1.0, 0.0).astype(jnp.bfloat16)
        to_cols = jnp.where(mid_col[...] == col_row[...], 1.0, 0.0).astype(jnp.bfloat16)
        m_parts = []
        for part in halves(m_ref[...]):
            turned = single(to_rows, part).astype(jnp.bfloat16)
            m_parts.append(single(turned, to_cols).astype(jnp.bfloat16))
        for start in range(0, cols_here, 256):
            x_high, x_low = halves(xc_ref[:, start : start + 256])
            right = single(m_parts[0], x_high) + single(m_parts[0], x_low) + single(m_parts[1], x_high)
            high, low = halves(right)
            high_ref[:, start : start + 256] = high
            low_ref[:, start : start + 256] = low

        @pl.when(has_panel)
        def _():
            at = pl.multiple_of(jnp.minimum(col_index, PANEL_BLOCKS - 1) * B, B)
            y_high, y_low = halves(y_ref[:, pl.ds(at, B)])
            high_ref[:, :B] = single(to_rows, y_high).astype(jnp.bfloat16)
            low_ref[:, :B] = single(to_rows, y_low).astype(jnp.bfloat16)

    left_high, left_low = halves(xr_ref[...].T)
    for start in range(0, cols_here, 256):
        high = high_ref[:, start : start + 256]
        low = low_ref[:, start : start + 256]
        out_ref[:, start : start + 256] = single(left_high, high) + single(left_high, low) + single(left_low, high)

    down = lax.broadcasted_iota(jnp.int32, (B, B), 0)
    along = lax.broadcasted_iota(jnp.int32, (B, B), 1)

    @pl.when(row_index == col_index % N_ROW)
    def _():
        upper_half = col_index // N_ROW
        rows = pl.ds(pl.multiple_of(upper_half * B, B), B)
        cols = pl.ds(pl.multiple_of(step * B, B), B)
        ridge = jnp.broadcast_to(damp_ref[pl.ds(col_index + N_COL * step, 1), :], (B, B))
        out_ref[rows, cols] = out_ref[rows, cols] + jnp.where(down == along, ridge, 0.0)

    @pl.when(step == 0)
    def _():
        product = out_ref[:B, :B]
        out_ref[:B, :] = jnp.zeros((B, cols_here), jnp.float32)

        @pl.when(has_panel & (row_index > col_index))
        def _():
            out_ref[:B, :B] = product

        @pl.when(has_panel & (row_index == col_index))
        def _():
            at = pl.multiple_of(jnp.minimum(col_index, PANEL_BLOCKS - 1) * B, B)
            out_ref[:B, :B] = u_ref[pl.ds(at, B), :].T


def tile(place, xr, xc, m, y, u, damp, mid, row, col):
    rows_here = xr.shape[1]
    cols_here = xc.shape[1]

    def whole(shape):
        return pl.BlockSpec(shape, lambda i: (0, 0))

    return pl.pallas_call(
        tile_kernel,
        grid=(rows_here // 256,),
        out_shape=jax.ShapeDtypeStruct((rows_here, cols_here), jnp.float32),
        in_specs=[
            pl.BlockSpec(memory_space=pltpu.SMEM),
            pl.BlockSpec((NEX, 256), lambda i: (0, i)),
            whole(xc.shape),
            whole(m.shape),
            whole(y.shape),
            whole(u.shape),
            whole(damp.shape),
            whole((NEX, 1)),
            whole((1, NEX)),
            whole((NEX, 1)),
            whole((1, NEX)),
        ],
        out_specs=pl.BlockSpec((256, cols_here), lambda i: (i, 0)),
        scratch_shapes=[pltpu.VMEM((NEX, cols_here), jnp.bfloat16)] * 2,
        compiler_params=pltpu.CompilerParams(vmem_limit_bytes=40 << 20),
        cost_estimate=pl.CostEstimate(flops=12_000_000_000, bytes_accessed=24_000_000, transcendentals=0),
        name="tile",
    )(
        place, xr, xc, m, y, u, damp, mid.reshape(-1, 1), mid.reshape(1, -1), row.reshape(-1, 1), col.reshape(1, -1)
    )


def swap(value, mask):
    devices = N_ROW * N_COL
    return lax.ppermute(value, ("row", "col"), [(i, i ^ mask) for i in range(devices)])


ROW_LOW, ROW_HIGH = (16, 32, 48), (64,)
COL_CORE, COL_LOW, COL_HIGH = (1,), (2, 4, 6), (8,)


def spread_out(value, phases):
    masks = [0]
    for phase in phases:
        value = jnp.concatenate([value] + [swap(value, mask) for mask in phase], 0)
        masks = [held ^ mask for mask in (0,) + phase for held in masks]
    return value, masks


def shards(activations, out_grads, proj_act, proj_grad, damping):
    row_index = lax.axis_index("row")
    col_index = lax.axis_index("col")
    me = row_index * N_COL + col_index
    act_sketch = jnp.dot(activations, proj_act, preferred_element_type=jnp.float32)
    grad_sketch = jnp.dot(out_grads, proj_grad, preferred_element_type=jnp.float32)
    here = activations.shape[0] // TOK_EX
    sketches = jnp.einsum(
        "eti,etj->eij",
        act_sketch.reshape(here, TOK_EX, SA),
        grad_sketch.reshape(here, TOK_EX, SG),
        precision=PRECISE,
    ) * (TOK_EX * NEX) ** (-0.5)
    sketches = sketches.reshape(here, F)
    rows_here = F // N_ROW
    cols_here = F // N_COL

    x_panel, masks = spread_out(sketches[:, :FINISHED], (ROW_LOW, ROW_HIGH, COL_HIGH, COL_LOW, COL_CORE))
    examples = jnp.arange(here, dtype=jnp.int32)
    mid_ids = ((me ^ jnp.array(masks, jnp.int32))[:, None] * here + examples).reshape(-1)

    by_rows = lax.all_to_all(
        sketches.reshape(here, rows_here // B, N_ROW, B), "row", split_axis=2, concat_axis=0, tiled=True
    ).reshape(N_ROW * here, rows_here)
    by_cols = lax.all_to_all(
        sketches.reshape(here, cols_here // B, N_COL, B), "col", split_axis=2, concat_axis=0, tiled=True
    ).reshape(N_COL * here, cols_here)
    xr = lax.all_gather(by_rows, "col", axis=0, tiled=True)
    xc = lax.all_gather(by_cols, "row", axis=0, tiled=True)
    positions = jnp.arange(N_ROW * N_COL, dtype=jnp.int32)
    col_ids = (positions[:, None] * here + examples).reshape(-1)
    row_ids = ((positions % N_ROW * N_COL + positions // N_ROW)[:, None] * here + examples).reshape(-1)

    damp_blocks = damping.reshape(F // B, B)
    m, y, u = chain(x_panel, x_panel.T, damp_blocks[:PANEL_BLOCKS], jnp.eye(NEX, dtype=jnp.float32))
    place = jnp.stack([row_index, col_index]).astype(jnp.int32)
    return tile(place, xr, xc, m, y, u, damp_blocks, mid_ids, row_ids, col_ids)


def solution(mesh):
    placed = (P(("row", "col"), None), P(("row", "col"), None), P(), P(), P())
    return jax.shard_map(
        shards, mesh=mesh, in_specs=placed, out_specs=P("row", "col"), check_vma=False
    )
```

time: 1270 us -> 267 us (0.21)
  waiting for transfers between devices: 680 us -> 93.9 us
  other arithmetic: 294 us -> 1.95 us
  matrix products: 123 us -> 4.23 us
  Pallas kernels: 0 us -> 66.6 us
  local copies, waits for them, and re-layouts: 109 us -> 44.1 us
    psum x6 -> x0, waiting for transfers between devices: 611 us -> none  [spread(): return lax.psum(kept, axis)]
    another operation x34 -> x1, other arithmetic: 237 us -> 0.07 us  [shards(): place = jnp.stack([row_index, col_index]).astype(jnp.int32)]
    ppermute x0 -> x9, waiting for transfers between devices: none -> 93.9 us  [swap(): lax.ppermute(value, ('row', 'col'), [(i, i ^ mask) for i in range(devices)])]
    dot_general x4 -> x1, matrix products: 83.9 us -> 0.79 us  [shards(): jnp.einsum('eti,etj->eij', act_sketch.reshape(here, TOK_EX, SA), grad_ske...]
    all_gather x2, waiting for transfers between devices: 69.5 us -> 0.01 us  [the longest x1 0.01 us: shards(): xc = lax.all_gather(by_cols, 'row', axis=0, tiled=True)]
    pallas_call x0 -> x2, Pallas kernels: none -> 66.6 us  [the longest x1 46.7 us: chain(): pl.pallas_call(functools.partial(chain_kernel, count), out_shape=(jax.Sha...]
    select_n x10 -> x0, other arithmetic: 37.1 us -> none  [the longest x6 31.9 us: spread(): jnp.where(lax.axis_index(axis) == source, value, 0).astype(value.dtype)]
    another operation x26 -> x0, matrix products: 36 us -> none  [the longest x14 31.5 us: shards(): solved = jax.scipy.linalg.solve_triangular(factor, columns.T, lower=True).T]
  transfers between devices with their start and end apart: 8 -> 11, of which waited for: 8 -> 7; matrix products, arithmetic and copies ran while one was open for 3% -> 11% of each run, Pallas kernels for 0% -> 18%
where the time goes in v1:
time: 267 us; the launch traced here: 266 us
  waiting for transfers between devices  93.9 us (35%)
  Pallas kernels  66.6 us (25%)
  local copies, waits for them, and re-layouts  44.1 us (17%)
  blocking collectives  31.4 us (12%)
  between operations  13.6 us (5%)
  starting transfers between devices  10.3 us (4%)
  matrix products  4.23 us (2%)
    ppermute x9, waiting for transfers between devices, swap(): lax.ppermute(value, ('row', 'col'), [(i, i ^ mask) for i in range(devices)])  93.9 us
    pallas_call x1, Pallas kernels, chain(): pl.pallas_call(functools.partial(chain_kernel, count), out_shape=(jax.Sha...  46.7 us
    pallas_call x1, Pallas kernels, tile(): pl.pallas_call(tile_kernel, grid=(rows_here // 256,), out_shape=jax.Shape...  19.9 us
    all_to_all x1, blocking collectives, shards(): lax.all_to_all(sketches.reshape(here, cols_here // B, N_COL, B), 'col', s...  18.2 us
    concatenate x5, local copies, waits for them, and re-layouts, spread_out(): value = jnp.concatenate([value] + [swap(value, mask) for mask in phase], 0)  18 us
    unnamed x38, local copies, waits for them, and re-layouts  17.9 us
    all_to_all x1, blocking collectives, shards(): lax.all_to_all(sketches.reshape(here, rows_here // B, N_ROW, B), 'row', s...  13.1 us
    ppermute x9, starting transfers between devices, swap(): lax.ppermute(value, ('row', 'col'), [(i, i ^ mask) for i in range(devices)])  10.2 us
  transfers between devices with their start and end apart: 11, of which 7 were waited for; matrix products, arithmetic and copies ran while one was open for 11% of the time, Pallas kernels for 18%

profile of v1, /device:TPU:1, one launch (start us, length us, event | category | flops | bytes accessed | tf_op | source)
XLA Modules:
  0.0 266.0 jit_solution(10225827618613168442)
XLA Ops:
  6.5 2.7 %fusion.5 = f32[256,128]{1,0:T(8,128)S(1)} fusion(bf16[256,4096]{1,0:T(8,128)(2,1)} %param.7, bf16[4096,128]{1,0:T(8,128)(2,1)} %param.9), kind=kOutput, calls=%fused_computation.22 | convolution fusion | flops 268435456 | bytes 3276800 | tf_op jit(solution)/shard_map/dot_general | solution.py:255
  9.3 0.1 copy-done.16
  9.4 0.7 fusion.4
  10.1 0.8 convolution_multiply_fusion
  10.9 0.2 copy.42
  11.2 18.2 %all_to_all.30 = f32[4,10,16,128]{3,0,1,2:T(4,128)S(1)} all-to-all(f32[4,10,16,128]{3,0,1,2:T(4,128)S(1)} %copy.42), channel_id=1, replica_groups=mesh['row'=8,'col'=16] {'col'}, dimensions={2} | all-to-all | bytes 655360 | tf_op jit(solution)/shard_map/all_to_all | solution.py:274
  29.4 0.8 copy.53
  30.3 0.2 copy.40
  30.5 13.1 %all_to_all.31 = f32[4,20,8,128]{3,0,1,2:T(4,128)S(1)} all-to-all(f32[4,20,8,128]{3,0,1,2:T(4,128)S(1)} %copy.40), channel_id=1, replica_groups=mesh['row'=8,'col'=16] {'row'}, dimensions={2} | all-to-all | bytes 655360 | tf_op jit(solution)/shard_map/all_to_all | solution.py:271
  43.7 0.8 copy.54
  44.5 5.4 %copy.44 = f32[4,160,128]{0,2,1:T(8,128)} copy(f32[4,160,128]{2,1,0:T(8,128)S(1)} %convolution_multiply_fusion) | data formatting | bytes 655360 | tf_op jit(solution)/shard_map/mul | solution.py:257
  50.0 1.1 slice.20
  51.1 0.9 collective-permute-start.2
  51.9 1.4 collective-permute-start.1
  53.3 1.1 collective-permute-start
  54.4 33.0 %collective-permute-done.2 = f32[4,1024]{0,1:T(8,128)S(1)} collective-permute-done((f32[4,1024]{0,1:T(8,128)S(1)}, f32[4,1024]{0,1:T(8,128)S(1)}, u32[]{:S(2)}, u32[]{:S(2)}) %collective-permute-start.2) | collective-permute-done | bytes 16416 | tf_op jit(solution)/shard_map/ppermute | solution.py:235
  87.4 0.9 collective-permute-done
  88.3 0.8 copy-done.15
  89.1 1.5 pad_maximum_fusion
  90.7 11.1 %collective-permute-done.3 = f32[16,1024]{0,1:T(8,128)} collective-permute-done((f32[16,1024]{0,1:T(8,128)S(1)}, f32[16,1024]{0,1:T(8,128)}, u32[]{:S(2)}, u32[]{:S(2)}) %collective-permute-start.3) | collective-permute-done | bytes 65568 | tf_op jit(solution)/shard_map/ppermute | solution.py:235
  101.8 2.5 concatenate.20
  104.4 1.9 collective-permute-start.4
  106.3 14.4 %collective-permute-done.4 = f32[32,1024]{0,1:T(8,128)} collective-permute-done((f32[32,1024]{0,1:T(8,128)}, f32[32,1024]{0,1:T(8,128)}, u32[]{:S(2)}, u32[]{:S(2)}) %collective-permute-start.4) | collective-permute-done | bytes 131104 | tf_op jit(solution)/shard_map/ppermute | solution.py:235
  120.7 2.7 %concatenate.21 = f32[64,1024]{0,1:T(8,128)} concatenate(f32[4,1024]{0,1:T(8,128)S(1)} %slice.20, f32[4,1024]{0,1:T(8,128)} %copy-done.15, f32[4,1024]{0,1:T(8,128)} %collective-permute-done.1, f32[4,1024]{0,1:T(8,128)S(1)} %collective-permute-done.2, f32[16,1024]{0,1:T(8,128)} %collective-permute-done.3, f32[32,1024]{0,1:T(8,128)} %collective-permute-done.4), dimensions={0} | concatenate | bytes 524288 | tf_op jit(solution)/shard_map/concatenate | solution.py:245
  123.4 2.9 %collective-permute-start.7 = (f32[64,1024]{0,1:T(8,128)}, f32[64,1024]{0,1:T(8,128)}, u32[]{:S(2)}, u32[]{:S(2)}) collective-permute-start(f32[64,1024]{0,1:T(8,128)} %concatenate.21), channel_id=1, source_target_pairs={{0,6},{1,7},{2,4},{3,5},{4,2},{5,3},{6,0},{7,1},{8,14},{9,15},{10,... | collective-permute-start | bytes 786440 | tf_op jit(solution)/shard_map/ppermute | solution.py:235
  126.3 0.5 collective-permute-start.6
  126.8 0.1 collective-permute-start.5
  127.0 32.1 %collective-permute-done.7 = f32[64,1024]{0,1:T(8,128)} collective-permute-done((f32[64,1024]{0,1:T(8,128)}, f32[64,1024]{0,1:T(8,128)}, u32[]{:S(2)}, u32[]{:S(2)}) %collective-permute-start.7) | collective-permute-done | bytes 262176 | tf_op jit(solution)/shard_map/ppermute | solution.py:235
  159.1 1.4 collective-permute-done.5
  160.4 4.6 %concatenate.22 = f32[256,1024]{0,1:T(8,128)} concatenate(f32[4,1024]{0,1:T(8,128)S(1)} %slice.20, f32[4,1024]{0,1:T(8,128)} %copy-done.15, f32[4,1024]{0,1:T(8,128)} %collective-permute-done.1, f32[4,1024]{0,1:T(8,128)S(1)} %collective-permute-done.2, f32[16,1024]{0,1:T(8,128)} %collective-permute-done.3, f32[32,1024]{0,1:T(8,128)} %collective-permute-done.4, ...), dimensions={0} | concatenate | bytes 2097152 | tf_op jit(solution)/shard_map/concatenate | solution.py:245
  165.1 1.4 collective-permute-start.8
  167.0 0.8 add.121.row_col
  168.0 1.1 collective-permute-done.8
  169.1 5.1 %concatenate.23 = f32[512,1024]{0,1:T(8,128)} concatenate(f32[4,1024]{0,1:T(8,128)} %copy-done.13, f32[4,1024]{0,1:T(8,128)} %copy-done.15, f32[4,1024]{0,1:T(8,128)} %collective-permute-done.1, f32[4,1024]{0,1:T(8,128)} %copy-done.14, f32[16,1024]{0,1:T(8,128)} %collective-permute-done.3, f32[32,1024]{0,1:T(8,128)} %collective-permute-done.4, ...), dimensions={0} | concatenate | bytes 4194304 | tf_op jit(solution)/shard_map/concatenate | solution.py:245
  174.2 2.9 %copy.45.x_ref = f32[512,1024]{1,0:T(8,128)} copy(f32[512,1024]{0,1:T(8,128)} %concatenate.23) | data formatting | bytes 4194304 | tf_op jit(solution)/shard_map/concatenate | solution.py:245
  177.2 1.6 copy-done.1
  178.8 1.6 copy-done.2
  180.3 46.7 %chain.1 = (f32[512,512]{1,0:T(8,128)S(1)}, f32[512,1024]{1,0:T(8,128)S(1)}, f32[1024,128]{1,0:T(8,128)S(1)}) custom-call(f32[512,1024]{1,0:T(8,128)S(1)} %copy-done.2, f32[1024,512]{1,0:T(8,128)S(1)} %bitcast.35, f32[8,128]{1,0:T(8,128)S(1)} %slice_bitcast_fusion.damp_ref, f32[512,512]{1,0:T(8,128)S(1)} %fusion.start_ref), custom_call_target="tpu_custom_call" | custom-call | flops 20000000000 | bytes 120000000 | tf_op jit(solution)/shard_map/chain/pallas_call | solution.py:122
  227.1 1.3 copy-done.7
  228.4 1.0 copy-done.9
  229.5 0.8 copy-done.11
  230.3 0.9 copy-done.3
  231.2 2.5 copy-done.5
  233.7 1.7 copy-done.6
  235.4 1.6 copy-done.8
  237.0 1.2 copy-done.10
  238.3 1.0 copy-done.12
  239.3 19.9 %tile.1 = f32[2560,1280]{1,0:T(8,128)} custom-call(s32[2]{0:T(128)S(1)} %pad_add_fusion.place_ref, f32[512,2560]{1,0:T(8,128)S(1)} %copy-done.5, f32[512,1280]{1,0:T(8,128)S(1)} %copy-done.6, f32[512,512]{1,0:T(8,128)S(1)} %copy-done.10, f32[512,1024]{1,0:T(8,128)S(1)} %copy-done.8, f32[1024,128]{1,0:T(8,128)S(1)} %copy-done.12, f32[160,128]{1,0:T(8,128)S(1)} %bitcast.36, ...), custom_call_target="tpu_custom_call" | custom-call | flops 12000000000 | bytes 24000000 | tf_op jit(solution)/shard_map/tile/pallas_call | solution.py:206
  (46 shorter events, 1.1 us)
Async XLA Ops:
  6.5 2.7 %copy-start = (bf16[256,4096]{1,0:T(8,128)(2,1)S(1)}, bf16[256,4096]{1,0:T(8,128)(2,1)}, u32[]{:S(2)}) copy-start(bf16[256,4096]{1,0:T(8,128)(2,1)} %param.6) | copy-start | bytes 6291460
  6.5 2.9 %copy-start.16 = (bf16[4096,160]{0,1:T(8,128)(2,1)S(1)}, bf16[4096,160]{0,1:T(8,128)(2,1)}, u32[]{:S(2)}) copy-start(bf16[4096,160]{0,1:T(8,128)(2,1)} %param.8) | copy-start | bytes 3932164
  6.5 223.7 %all-gather.5.cloned.1.call-start = ((), (), s32[]{:S(2)}) async-start(), calls=%async_computation.3 | async-start | bytes 2949120 | tf_op jit(solution)/shard_map/all_gather | solution.py:278
  30.3 200.0 %all-gather.3.cloned.1.call-start = ((), (), s32[]{:S(2)}) async-start(), calls=%async_computation.2 | async-start | bytes 5570560 | tf_op jit(solution)/shard_map/all_gather | solution.py:277
  51.0 109.4 %copy-start.13 = (f32[4,1024]{0,1:T(8,128)}, f32[4,1024]{0,1:T(8,128)S(1)}, u32[]{:S(2)}) copy-start(f32[4,1024]{0,1:T(8,128)S(1)} %slice.20) | copy-start | bytes 49156
  51.1 36.3 %collective-permute-start.2 = (f32[4,1024]{0,1:T(8,128)S(1)}, f32[4,1024]{0,1:T(8,128)S(1)}, u32[]{:S(2)}, u32[]{:S(2)}) collective-permute-start(f32[4,1024]{0,1:T(8,128)S(1)} %slice.20), channel_id=1, source_target_pairs={{0,48},{1,49},{2,50},{3,51},{4,52},{5,53},{6,54},{7,55},{8,56},{9,... | collective-permute-start | bytes 49160 | tf_op jit(solution)/shard_map/ppermute | solution.py:235
  51.9 35.5 %collective-permute-start.1 = (f32[4,1024]{0,1:T(8,128)S(1)}, f32[4,1024]{0,1:T(8,128)}, u32[]{:S(2)}, u32[]{:S(2)}) collective-permute-start(f32[4,1024]{0,1:T(8,128)S(1)} %slice.20), channel_id=1, source_target_pairs={{0,32},{1,33},{2,34},{3,35},{4,36},{5,37},{6,38},{7,39},{8,40},{9,... | collective-permute-start | bytes 49160 | tf_op jit(solution)/shard_map/ppermute | solution.py:235
  53.3 35.0 %collective-permute-start = (f32[4,1024]{0,1:T(8,128)S(1)}, f32[4,1024]{0,1:T(8,128)S(1)}, u32[]{:S(2)}, u32[]{:S(2)}) collective-permute-start(f32[4,1024]{0,1:T(8,128)S(1)} %slice.20), channel_id=1, source_target_pairs={{0,16},{1,17},{2,18},{3,19},{4,20},{5,21},{6,22},{7,23},{8,24},{9,... | collective-permute-start | bytes 49160 | tf_op jit(solution)/shard_map/ppermute | solution.py:235
  87.4 77.7 %copy-start.14 = (f32[4,1024]{0,1:T(8,128)}, f32[4,1024]{0,1:T(8,128)S(1)}, u32[]{:S(2)}) copy-start(f32[4,1024]{0,1:T(8,128)S(1)} %collective-permute-done.2) | copy-start | bytes 49156
  88.3 0.8 copy-start.15
  90.6 11.2 %collective-permute-start.3 = (f32[16,1024]{0,1:T(8,128)S(1)}, f32[16,1024]{0,1:T(8,128)}, u32[]{:S(2)}, u32[]{:S(2)}) collective-permute-start(f32[16,1024]{0,1:T(8,128)S(1)} %pad_maximum_fusion), channel_id=1, source_target_pairs={{0,64},{1,65},{2,66},{3,67},{4,68},{5,69},{6,70},{7,71},{8,72},{9,... | collective-permute-start | bytes 196616 | tf_op jit(solution)/shard_map/ppermute | solution.py:235
  104.4 22.5 %copy-start.17 = (s32[128]{0:T(128)S(1)}, s32[128]{0:T(128)}, u32[]{:S(2)}) copy-start(s32[128]{0:T(128)} %constant.49.clone) | copy-start | bytes 1540
  104.4 16.3 %collective-permute-start.4 = (f32[32,1024]{0,1:T(8,128)}, f32[32,1024]{0,1:T(8,128)}, u32[]{:S(2)}, u32[]{:S(2)}) collective-permute-start(f32[32,1024]{0,1:T(8,128)} %concatenate.20), channel_id=1, source_target_pairs={{0,8},{1,9},{2,10},{3,11},{4,12},{5,13},{6,14},{7,15},{8,0},{9,1},... | collective-permute-start | bytes 393224 | tf_op jit(solution)/shard_map/ppermute | solution.py:235
  123.4 35.6 %collective-permute-start.7 = (f32[64,1024]{0,1:T(8,128)}, f32[64,1024]{0,1:T(8,128)}, u32[]{:S(2)}, u32[]{:S(2)}) collective-permute-start(f32[64,1024]{0,1:T(8,128)} %concatenate.21), channel_id=1, source_target_pairs={{0,6},{1,7},{2,4},{3,5},{4,2},{5,3},{6,0},{7,1},{8,14},{9,15},{10,... | collective-permute-start | bytes 786440 | tf_op jit(solution)/shard_map/ppermute | solution.py:235
  126.3 32.7 %collective-permute-start.6 = (f32[64,1024]{0,1:T(8,128)}, f32[64,1024]{0,1:T(8,128)}, u32[]{:S(2)}, u32[]{:S(2)}) collective-permute-start(f32[64,1024]{0,1:T(8,128)} %concatenate.21), channel_id=1, source_target_pairs={{0,4},{1,5},{2,6},{3,7},{4,0},{5,1},{6,2},{7,3},{8,12},{9,13},{10,... | collective-permute-start | bytes 786440 | tf_op jit(solution)/shard_map/ppermute | solution.py:235
  126.8 33.6 %collective-permute-start.5 = (f32[64,1024]{0,1:T(8,128)}, f32[64,1024]{0,1:T(8,128)}, u32[]{:S(2)}, u32[]{:S(2)}) collective-permute-start(f32[64,1024]{0,1:T(8,128)} %concatenate.21), channel_id=1, source_target_pairs={{0,2},{1,3},{2,0},{3,1},{4,6},{5,7},{6,4},{7,5},{8,10},{9,11},{10,... | collective-permute-start | bytes 786440 | tf_op jit(solution)/shard_map/ppermute | solution.py:235
  127.0 41.0 %copy-start.4 = (f32[20480]{0:T(1024)S(1)}, f32[20480]{0:T(1024)}, u32[]{:S(2)}) copy-start(f32[20480]{0:T(1024)} %param.10) | copy-start | bytes 245764
  165.1 4.0 %collective-permute-start.8 = (f32[256,1024]{0,1:T(8,128)}, f32[256,1024]{0,1:T(8,128)}, u32[]{:S(2)}, u32[]{:S(2)}) collective-permute-start(f32[256,1024]{0,1:T(8,128)} %concatenate.22), channel_id=1, source_target_pairs={{0,1},{1,0},{2,3},{3,2},{4,5},{5,4},{6,7},{7,6},{8,9},{9,8},{10,11... | collective-permute-start | bytes 3145736 | tf_op jit(solution)/shard_map/ppermute | solution.py:235
  177.2 1.6 copy-start.1
  178.8 1.6 copy-start.2
  227.1 1.3 copy-start.7
  228.4 1.0 copy-start.9
  229.5 0.8 copy-start.11
  230.3 1.0 copy-start.3
  231.2 2.5 copy-start.5
  233.7 1.7 copy-start.6
  235.4 1.6 copy-start.8
  237.0 1.2 copy-start.10
  238.3 1.0 copy-start.12
Sparse Core Ops, SparseCore 0:
  30.4 60.8 all-gather.4
  93.7 68.4 all-gather.2

commit v2 on v1

v2 whole, which is shorter than its diff:
```python
import functools

import jax
import jax.numpy as jnp
from jax import lax
from jax.experimental import pallas as pl
from jax.experimental.pallas import tpu as pltpu
from jax.sharding import PartitionSpec as P

SA = 160
SG = 128
TOK_EX = 64
B = 128
PW = 512
PANELS = 2
NEX = 512
F = SA * SG
N_ROW = 8
N_COL = 16
FINISHED = PW * PANELS
PANEL_BLOCKS = FINISHED // B
CALLS = (2, 3, 3)
VMEM = 60 << 20
ROW_BLOCKS = SA // N_ROW
COL_BLOCKS = SA // N_COL

PRECISE = lax.Precision.HIGHEST


def contract(left, right, left_dim, right_dim):
    return lax.dot_general(
        left,
        right,
        (((left_dim,), (right_dim,)), ((), ())),
        precision=PRECISE,
        preferred_element_type=jnp.float32,
    )


def single(left, right):
    return jnp.dot(left, right, preferred_element_type=jnp.float32)


def halves(value):
    high = value.astype(jnp.bfloat16)
    return high, (value - high.astype(jnp.float32)).astype(jnp.bfloat16)


def eliminate(square):
    sub = lax.broadcasted_iota(jnp.int32, (8, B), 0)
    lane = lax.broadcasted_iota(jnp.int32, (8, B), 1)
    tiles = [square[8 * t : 8 * t + 8, :] for t in range(B // 8)]
    for group in range(B // 8):
        first = 8 * group
        cols = {}
        for t in range(group, B // 8):
            for w in range(8):
                cols[t, w] = jnp.broadcast_to(tiles[t][:, first + w : first + w + 1], (8, B))
        scale = None
        for w in range(8):
            here = lane == first + w
            pivot = jnp.broadcast_to(cols[group, w][w : w + 1, :], (8, B))
            later = [jnp.broadcast_to(cols[group, v][w : w + 1, :], (8, B)) for v in range(w + 1, 8)]
            inverse = 1.0 / pivot
            row = jnp.where(here, 1.0, jnp.broadcast_to(tiles[group][w : w + 1, :], (8, B)))
            for t in range(group, B // 8):
                column = cols[t, w]
                cleared = here
                if t == group:
                    column = jnp.where(sub > w, column, 0.0)
                    cleared = here & (sub > w)
                ratio = column * inverse
                for v in range(w + 1, 8):
                    cols[t, v] = cols[t, v] - ratio * later[v - w - 1]
                tiles[t] = jnp.where(cleared, 0.0, tiles[t]) - ratio * row
            root = lax.rsqrt(pivot)
            scale = root if scale is None else jnp.where(sub >= w, root, scale)
        tiles[group] = jnp.where(lane == sub + first, scale, tiles[group] * scale)
    lower = [jnp.where(lane <= sub + 8 * t, tile, 0.0) for t, tile in enumerate(tiles)]
    upper = [
        jnp.where(lane > sub + 8 * t, tile, jnp.where(lane == sub + 8 * t, 1.0 / tile, 0.0))
        for t, tile in enumerate(tiles)
    ]
    return jnp.concatenate(upper, 0), jnp.concatenate(lower, 0)


def chain_kernel(first_block, count, pieces, *refs):
    x_refs, refs = refs[:pieces], refs[pieces:]
    if first_block == 0:
        damp_ref, m_ref, y_ref, u_ref, s_ref, last_ref = refs
    else:
        damp_ref, start_ref, m_ref, y_ref, u_ref, s_ref, last_ref = refs
    down = lax.broadcasted_iota(jnp.int32, (B, B), 0)
    along = lax.broadcasted_iota(jnp.int32, (B, B), 1)

    def ridge(k):
        return jnp.where(down == along, jnp.broadcast_to(damp_ref[pl.ds(k, 1), :], (B, B)), 0.0)

    def columns(k):
        return jnp.concatenate([ref[k] for ref in x_refs], 0)

    block = columns(first_block)
    if first_block == 0:
        one = lax.broadcasted_iota(jnp.int32, (NEX, NEX), 0) == lax.broadcasted_iota(jnp.int32, (NEX, NEX), 1)
        m_ref[...] = jnp.where(one, 1.0, 0.0)
        s_ref[...] = contract(block.T, block, 1, 0) + ridge(first_block)
    else:
        m_ref[...] = start_ref[...]
        s_ref[...] = contract(block.T, contract(start_ref[...], block, 1, 0), 1, 0) + ridge(first_block)
    last_ref[...] = jnp.zeros_like(last_ref)

    def body(k, carry):
        here = first_block + k
        there = first_block + jnp.minimum(k + 1, count - 1)
        square = s_ref[...]
        last = last_ref[...]
        m_now = m_ref[...] - contract(last, last, 1, 1)
        m_ref[...] = m_now
        following = columns(there)
        both = contract(m_now, jnp.concatenate([columns(here), following], 1), 1, 0)
        ahead = contract(following.T, both, 1, 0)
        upper, inverse = eliminate(square)
        below = contract(ahead[:, :B], inverse, 1, 1)
        s_ref[...] = ahead[:, B:] - contract(below, below, 1, 1) + ridge(there)
        y_now = contract(both[:, :B], inverse, 1, 1)
        last_ref[...] = y_now
        y_ref[k] = y_now
        u_ref[k] = upper
        return carry

    lax.fori_loop(0, count, body, 0)
    last = last_ref[...]
    m_ref[...] = m_ref[...] - contract(last, last, 1, 1)


def chain(x, damp, first_block, count, start):
    return pl.pallas_call(
        functools.partial(chain_kernel, first_block, count, len(x)),
        out_shape=(
            jax.ShapeDtypeStruct((NEX, NEX), jnp.float32),
            jax.ShapeDtypeStruct((count, NEX, B), jnp.float32),
            jax.ShapeDtypeStruct((count, B, B), jnp.float32),
        ),
        scratch_shapes=[pltpu.VMEM((B, B), jnp.float32), pltpu.VMEM((NEX, B), jnp.float32)],
        compiler_params=pltpu.CompilerParams(vmem_limit_bytes=VMEM),
        cost_estimate=pl.CostEstimate(flops=6_000_000_000 * count, bytes_accessed=16_000_000 * count, transcendentals=0),
        name="chain",
    )(*x, damp, *(() if start is None else (start,)))


def tile_kernel(place_ref, *refs):
    xr_refs = refs[:8]
    xc_ref, m_ref = refs[8:10]
    y_refs, u_refs = refs[10 : 10 + len(CALLS)], refs[10 + len(CALLS) : 10 + 2 * len(CALLS)]
    damp_ref, row_ids, col_ids, out_ref, high_ref, low_ref = refs[10 + 2 * len(CALLS) :]
    step = pl.program_id(0)
    row_index = place_ref[0]
    col_index = place_ref[1]
    cols_here = out_ref.shape[1]
    starts = [sum(CALLS[:call]) for call in range(len(CALLS))]
    in_call = [jnp.clip(col_index - start, 0, count - 1) for start, count in zip(starts, CALLS)]
    chosen = [(col_index >= start) & (col_index < start + count) for start, count in zip(starts, CALLS)]

    @pl.when(step == 0)
    def _():
        to_cols = jnp.where(row_ids[...] == col_ids[...], 1.0, 0.0).astype(jnp.bfloat16)
        m_high, m_low = [single(part, to_cols).astype(jnp.bfloat16) for part in halves(m_ref[...])]
        for start in range(0, COL_BLOCKS, 2):
            columns = [
                jnp.concatenate([xc_ref[piece, start + k] for piece in range(xc_ref.shape[0])], 0) for k in range(2)
            ]
            x_high, x_low = halves(jnp.concatenate(columns, 1))
            right = single(m_high, x_high) + single(m_high, x_low) + single(m_low, x_high)
            high, low = halves(right)
            high_ref[:, start * B : (start + 2) * B] = high
            low_ref[:, start * B : (start + 2) * B] = low

        for call, y_ref in enumerate(y_refs):

            @pl.when(chosen[call])
            def _(call=call, y_ref=y_ref):
                high, low = halves(y_ref[in_call[call]])
                high_ref[:, :B] = high
                low_ref[:, :B] = low

    left = jnp.concatenate([jnp.concatenate([ref[k] for ref in xr_refs], 0).T for k in range(2)], 0)
    left_high, left_low = halves(left)
    for start in range(0, cols_here, 256):
        high = high_ref[:, start : start + 256]
        low = low_ref[:, start : start + 256]
        out_ref[:, start : start + 256] = single(left_high, high) + single(left_high, low) + single(left_low, high)

    down = lax.broadcasted_iota(jnp.int32, (B, B), 0)
    along = lax.broadcasted_iota(jnp.int32, (B, B), 1)

    @pl.when(row_index == col_index % N_ROW)
    def _():
        rows = pl.ds(pl.multiple_of(col_index // N_ROW * B, B), B)
        cols = pl.ds(pl.multiple_of(step * B, B), B)
        ridge = jnp.broadcast_to(damp_ref[pl.ds(col_index + N_COL * step, 1), :], (B, B))
        out_ref[rows, cols] = out_ref[rows, cols] + jnp.where(down == along, ridge, 0.0)

    @pl.when(step == 0)
    def _():
        product = out_ref[:B, :B]
        out_ref[:B, :] = jnp.zeros((B, cols_here), jnp.float32)

        @pl.when((col_index < PANEL_BLOCKS) & (row_index > col_index))
        def _():
            out_ref[:B, :B] = product

        for call, u_ref in enumerate(u_refs):

            @pl.when(chosen[call] & (row_index == col_index))
            def _(call=call, u_ref=u_ref):
                out_ref[:B, :B] = u_ref[in_call[call]].T


def tile(place, xr, xc, m, y, u, damp, row_ids, col_ids):
    rows_here, cols_here = ROW_BLOCKS * B, COL_BLOCKS * B

    def whole(value):
        return pl.BlockSpec(value.shape, lambda i: (0,) * value.ndim)

    rest = (xc, m, *y, *u, damp, row_ids.reshape(-1, 1), col_ids.reshape(1, -1))
    return pl.pallas_call(
        tile_kernel,
        grid=(ROW_BLOCKS // 2,),
        out_shape=jax.ShapeDtypeStruct((rows_here, cols_here), jnp.float32),
        in_specs=[pl.BlockSpec(memory_space=pltpu.SMEM)]
        + [pl.BlockSpec((2,) + piece.shape[1:], lambda i: (i, 0, 0)) for piece in xr]
        + [whole(value) for value in rest],
        out_specs=pl.BlockSpec((2 * B, cols_here), lambda i: (i, 0)),
        scratch_shapes=[pltpu.VMEM((NEX, cols_here), jnp.bfloat16)] * 2,
        compiler_params=pltpu.CompilerParams(vmem_limit_bytes=VMEM),
        cost_estimate=pl.CostEstimate(flops=12_000_000_000, bytes_accessed=24_000_000, transcendentals=0),
        name="tile",
    )(place, *xr, *rest)


def moved(value, target):
    pairs = [(row * N_COL + col, target(row, col)) for row in range(N_ROW) for col in range(N_COL)]
    return lax.ppermute(value, ("row", "col"), pairs)


def swapped(value, mask):
    return moved(value, lambda row, col: row * N_COL + (col ^ mask))


FAR, RING, CORE = 8, (2, 4, 6), 1


def shards(activations, out_grads, proj_act, proj_grad, damping):
    row_index = lax.axis_index("row")
    col_index = lax.axis_index("col")
    act_sketch = jnp.dot(activations, proj_act, preferred_element_type=jnp.float32)
    grad_sketch = jnp.dot(out_grads, proj_grad, preferred_element_type=jnp.float32)
    here = activations.shape[0] // TOK_EX
    sketches = jnp.einsum(
        "eti,etj->eij",
        act_sketch.reshape(here, TOK_EX, SA),
        grad_sketch.reshape(here, TOK_EX, SG),
        precision=PRECISE,
    ) * (TOK_EX * NEX) ** (-0.5)

    for_rows = sketches.reshape(here, ROW_BLOCKS, N_ROW, B).transpose(2, 1, 0, 3)
    for_panel = jnp.broadcast_to(
        sketches[:, :PANEL_BLOCKS].transpose(1, 0, 2), (N_ROW, PANEL_BLOCKS, here, B)
    )
    parcels = lax.all_to_all(jnp.concatenate([for_rows, for_panel], 1), "row", split_axis=0, concat_axis=0)
    group = N_ROW * here
    parcels = parcels.transpose(1, 0, 2, 3).reshape(ROW_BLOCKS + PANEL_BLOCKS, group, B)
    rows = parcels[:ROW_BLOCKS]
    panel = parcels[ROW_BLOCKS:]

    parity = col_index % 2
    split = rows.reshape(COL_BLOCKS, 2, group, B)
    near = lax.dynamic_index_in_dim(split, parity, 1, keepdims=False)
    other = lax.dynamic_index_in_dim(split, 1 - parity, 1, keepdims=False)
    panel_far = swapped(panel, FAR)
    near = moved(near, lambda row, col: col // 2 * N_COL + row + N_ROW * (col % 2))
    other = moved(other, lambda row, col: col // 2 * N_COL + row + N_ROW * (1 - col % 2))
    rows_far = swapped(rows, FAR)
    panel = jnp.concatenate([panel, panel_far], 1)
    panels = [panel] + [swapped(panel, mask) for mask in RING]
    panels = panels + [swapped(piece, CORE) for piece in panels]

    damp_blocks = damping.reshape(SA, B)
    m, y0, u0 = chain(panels, damp_blocks, 0, CALLS[0], None)
    m, near, other, rows, rows_far = lax.optimization_barrier((m, near, other, rows, rows_far))
    xc = lax.all_gather(jnp.concatenate([near, other], 1), "row", axis=0)
    rows = jnp.concatenate([rows, rows_far], 1)
    pieces = [rows] + [swapped(rows, mask) for mask in RING]
    m, y1, u1 = chain(panels, damp_blocks, CALLS[0], CALLS[1], m)
    m, pieces = lax.optimization_barrier((m, pieces))
    pieces = pieces + [swapped(piece, CORE) for piece in pieces]
    m, y2, u2 = chain(panels, damp_blocks, CALLS[0] + CALLS[1], CALLS[2], m)

    ex = jnp.arange(here, dtype=jnp.int32)
    line = jnp.arange(N_ROW, dtype=jnp.int32)[:, None] * N_COL
    masks = [core ^ ring ^ far for core in (0, CORE) for ring in (0,) + RING for far in (0, FAR)]
    row_ids = (line + (col_index ^ jnp.array(masks, jnp.int32))[:, None, None])[..., None] * here + ex
    turn = col_index // N_ROW ^ jnp.arange(2, dtype=jnp.int32)
    sources = 2 * jnp.arange(N_ROW, dtype=jnp.int32)[:, None] + turn
    col_ids = (line + sources[:, :, None, None])[..., None] * here + ex
    place = jnp.stack([row_index, col_index]).astype(jnp.int32)
    return tile(place, pieces, xc, m, (y0, y1, y2), (u0, u1, u2), damp_blocks, row_ids.reshape(-1), col_ids.reshape(-1))


def solution(mesh):
    placed = (P(("row", "col"), None), P(("row", "col"), None), P(), P(), P())
    return jax.shard_map(
        shards, mesh=mesh, in_specs=placed, out_specs=P("row", "col"), check_vma=False
    )
```

time: 267 us -> 164 us (0.61)
  waiting for transfers between devices: 93.9 us -> 14 us
  local copies, waits for them, and re-layouts: 44.1 us -> 2.84 us
  starting transfers between devices: 10.3 us -> 28.9 us
  blocking collectives: 31.4 us -> 14.6 us
  Pallas kernels: 66.6 us -> 83.2 us
    ppermute x9 -> x18, waiting for transfers between devices: 93.9 us -> 14 us  [moved(): return lax.ppermute(value, ('row', 'col'), pairs)]
    ppermute x9 -> x18, starting transfers between devices: 10.2 us -> 28.9 us  [moved(): return lax.ppermute(value, ('row', 'col'), pairs)]
    concatenate x5 -> x1, local copies, waits for them, and re-layouts: 18 us -> 0.02 us  [shards(): rows = jnp.concatenate([rows, rows_far], 1)]
    unnamed x38 -> x19, local copies, waits for them, and re-layouts: 17.9 us -> 0.89 us
    all_to_all x2 -> x1, blocking collectives: 31.4 us -> 14.6 us  [shards(): lax.all_to_all(jnp.concatenate([for_rows, for_panel], 1), 'row', split_ax...]
    pallas_call x2 -> x4, Pallas kernels: 66.6 us -> 83.2 us  [the longest x3 61.4 us: chain(): pl.pallas_call(functools.partial(chain_kernel, first_block, count, len(x)...]
    mul x1 -> x0, local copies, waits for them, and re-layouts: 5.44 us -> none  [shards(): jnp.einsum('eti,etj->eij', act_sketch.reshape(here, TOK_EX, SA), grad_ske...]
  transfers between devices with their start and end apart: 11 -> 19, of which waited for: 7 -> 3; matrix products, arithmetic and copies ran while one was open for 11% -> 2% of each run, Pallas kernels for 18% -> 38%
where the time goes in v2:
time: 164 us; the launch traced here: 163 us
  Pallas kernels  83.2 us (51%)
  starting transfers between devices  28.9 us (18%)
  blocking collectives  14.6 us (9%)
  waiting for transfers between devices  14 us (9%)
  between operations  13.7 us (8%)
  matrix products  4.23 us (3%)
  local copies, waits for them, and re-layouts  2.84 us (2%)
  other arithmetic  1.95 us (1%)
    pallas_call x3, Pallas kernels, chain(): pl.pallas_call(functools.partial(chain_kernel, first_block, count, len(x)...  61.4 us
    ppermute x18, starting transfers between devices, moved(): return lax.ppermute(value, ('row', 'col'), pairs)  28.9 us
    pallas_call x1, Pallas kernels, tile(): pl.pallas_call(tile_kernel, grid=(ROW_BLOCKS // 2,), out_shape=jax.ShapeD...  21.7 us
    all_to_all x1, blocking collectives, shards(): lax.all_to_all(jnp.concatenate([for_rows, for_panel], 1), 'row', split_ax...  14.6 us
    ppermute x18, waiting for transfers between devices, moved(): return lax.ppermute(value, ('row', 'col'), pairs)  14 us
  transfers between devices with their start and end apart: 19, of which 3 were waited for; matrix products, arithmetic and copies ran while one was open for 2% of the time, Pallas kernels for 38%

profile of v2, /device:TPU:1, one launch (start us, length us, event | category | flops | bytes accessed | tf_op | source)
XLA Modules:
  0.0 163.4 jit_solution(16588404259505141390)
XLA Ops:
  6.5 2.7 %fusion.1 = f32[256,128]{1,0:T(8,128)S(1)} fusion(bf16[256,4096]{1,0:T(8,128)(2,1)} %param.7, bf16[4096,128]{1,0:T(8,128)(2,1)} %param.9), kind=kOutput, calls=%fused_computation.21 | convolution fusion | flops 268435456 | bytes 3276800 | tf_op jit(solution)/shard_map/dot_general | solution.py:257
  9.3 0.1 copy-done.3
  9.4 0.7 fusion
  10.1 0.8 convolution_multiply_fusion
  11.0 0.2 copy.33
  11.2 0.1 pad_maximum_fusion
  11.3 14.6 %all_to_all.5 = f32[8,28,4,128]{3,2,1,0:T(4,128)S(1)} all-to-all(f32[8,28,4,128]{3,2,1,0:T(4,128)S(1)} %pad_maximum_fusion), channel_id=1, replica_groups=mesh['row'=8,'col'=16] {'row'}, dimensions={0} | all-to-all | bytes 917504 | tf_op jit(solution)/shard_map/all_to_all | solution.py:270
  26.0 3.4 %collective-permute-start = (f32[8,32,128]{2,1,0:T(8,128)S(1)}, f32[8,32,128]{2,1,0:T(8,128)S(1)}, u32[]{:S(2)}, u32[]{:S(2)}) collective-permute-start(f32[8,32,128]{2,1,0:T(8,128)S(1)} %bitcast.42), channel_id=1, source_target_pairs={{0,8},{1,9},{2,10},{3,11},{4,12},{5,13},{6,14},{7,15},{8,0},{9,1},... | collective-permute-start | bytes 393224 | tf_op jit(solution)/shard_map/ppermute | solution.py:243
  29.4 2.4 %collective-permute-done = f32[8,32,128]{2,1,0:T(8,128)S(1)} collective-permute-done((f32[8,32,128]{2,1,0:T(8,128)S(1)}, f32[8,32,128]{2,1,0:T(8,128)S(1)}, u32[]{:S(2)}, u32[]{:S(2)}) %collective-permute-start) | collective-permute-done | bytes 131104 | tf_op jit(solution)/shard_map/ppermute | solution.py:243
  31.8 2.8 %collective-permute-start.3 = (f32[8,64,128]{2,1,0:T(8,128)S(1)}, f32[8,64,128]{2,1,0:T(8,128)S(1)}, u32[]{:S(2)}, u32[]{:S(2)}) collective-permute-start(f32[8,64,128]{2,1,0:T(8,128)S(1)} %pad_maximum_fusion.2.refs_0_), channel_id=1, source_target_pairs={{0,6},{1,7},{2,4},{3,5},{4,2},{5,3},{6,0},{7,1},{8,14},{9,15},{10,... | collective-permute-start | bytes 786440 | tf_op jit(solution)/shard_map/ppermute | solution.py:243
  34.6 0.3 collective-permute-start.2
  35.0 0.3 collective-permute-start.1
  35.3 0.1 broadcast_add_fusion
  35.4 3.2 %collective-permute-start.4 = (f32[8,64,128]{2,1,0:T(8,128)S(1)}, f32[8,64,128]{2,1,0:T(8,128)S(1)}, u32[]{:S(2)}, u32[]{:S(2)}) collective-permute-start(f32[8,64,128]{2,1,0:T(8,128)S(1)} %pad_maximum_fusion.2.refs_0_), channel_id=1, source_target_pairs={{0,1},{1,0},{2,3},{3,2},{4,5},{5,4},{6,7},{7,6},{8,9},{9,8},{10,11... | collective-permute-start | bytes 786440 | tf_op jit(solution)/shard_map/ppermute | solution.py:243
  38.6 7.2 %collective-permute-done.3.refs_3_ = f32[8,64,128]{2,1,0:T(8,128)S(1)} collective-permute-done((f32[8,64,128]{2,1,0:T(8,128)S(1)}, f32[8,64,128]{2,1,0:T(8,128)S(1)}, u32[]{:S(2)}, u32[]{:S(2)}) %collective-permute-start.3) | collective-permute-done | bytes 262176 | tf_op jit(solution)/shard_map/ppermute | solution.py:243
  45.8 1.3 collective-permute-start.7
  47.1 0.0 collective-permute-done.2.refs_2_
  47.1 0.7 collective-permute-start.6
  47.8 0.0 collective-permute-done.1.refs_1_
  47.8 0.5 collective-permute-start.5
  48.3 0.1 add_multiply_fusion
  48.4 0.1 copy.28
  48.5 0.1 collective-permute-start.9
  48.6 5.3 %collective-permute-start.8 = (f32[10,32,128]{2,1,0:T(8,128)S(1)}, f32[10,32,128]{2,1,0:T(8,128)S(1)}, u32[]{:S(2)}, u32[]{:S(2)}) collective-permute-start(f32[10,32,128]{2,1,0:T(8,128)S(1)} %get-tuple-element.44), channel_id=1, source_target_pairs={{0,0},{1,8},{2,16},{3,24},{4,32},{5,40},{6,48},{7,56},{8,64},{9,72... | collective-permute-start | bytes 491528 | tf_op jit(solution)/shard_map/ppermute | solution.py:243
  54.0 0.7 copy-done.7
  54.7 2.8 %collective-permute-start.10 = (f32[20,32,128]{2,1,0:T(8,128)S(1)}, f32[20,32,128]{2,1,0:T(8,128)S(1)}, u32[]{:S(2)}, u32[]{:S(2)}) collective-permute-start(f32[20,32,128]{2,1,0:T(8,128)S(1)} %bitcast.35), channel_id=1, source_target_pairs={{0,8},{1,9},{2,10},{3,11},{4,12},{5,13},{6,14},{7,15},{8,0},{9,1},... | collective-permute-start | bytes 983048 | tf_op jit(solution)/shard_map/ppermute | solution.py:243
  57.4 0.0 copy-start.8
  57.5 15.5 %chain.3 = (f32[512,512]{1,0:T(8,128)}, f32[2,512,128]{2,1,0:T(8,128)}, f32[2,128,128]{2,1,0:T(8,128)}) custom-call(f32[8,64,128]{2,1,0:T(8,128)} %copy-done.1, f32[8,64,128]{2,1,0:T(8,128)} %collective-permute-done.1.refs_1_, f32[8,64,128]{2,1,0:T(8,128)} %collective-permute-done.2.refs_2_, f32[8,64,128]{2,1,0:T(8,128)} %copy-done.5, ...), custom_call_target="tpu_custom_call" | custom-call | flops 12000000000 | bytes 32000000 | tf_op jit(solution)/shard_map/chain/pallas_call | solution.py:137
  73.0 0.8 pad_maximum_fusion.1
  73.8 0.0 all-gather.3.cloned.1.call-update
  73.8 0.1 iota_add_fusion
  73.9 0.7 add.139.refs_18_
  74.6 0.1 add_multiply_fusion.1
  74.7 0.1 iota_add_fusion.1
  74.7 0.8 add.140.refs_17_
  75.6 0.7 pad_add_fusion.place_ref
  76.3 4.5 %collective-permute-start.13 = (f32[20,64,128]{2,1,0:T(8,128)S(1)}, f32[20,64,128]{2,1,0:T(8,128)S(1)}, u32[]{:S(2)}, u32[]{:S(2)}) collective-permute-start(f32[20,64,128]{2,1,0:T(8,128)S(1)} %constant_dynamic-update-slice_fusion.refs_0_), channel_id=1, source_target_pairs={{0,6},{1,7},{2,4},{3,5},{4,2},{5,3},{6,0},{7,1},{8,14},{9,15},{10,... | collective-permute-start | bytes 1966088 | tf_op jit(solution)/shard_map/ppermute | solution.py:243
  80.8 0.6 collective-permute-start.12
  81.4 0.1 collective-permute-start.11
  81.5 23.0 %chain.4 = (f32[512,512]{1,0:T(8,128)}, f32[3,512,128]{2,1,0:T(8,128)}, f32[3,128,128]{2,1,0:T(8,128)}) custom-call(f32[8,64,128]{2,1,0:T(8,128)} %copy-done.1, f32[8,64,128]{2,1,0:T(8,128)} %collective-permute-done.1.refs_1_, f32[8,64,128]{2,1,0:T(8,128)} %collective-permute-done.2.refs_2_, f32[8,64,128]{2,1,0:T(8,128)} %copy-done.5, ...), custom_call_target="tpu_custom_call" | custom-call | flops 17999998976 | bytes 48000000 | tf_op jit(solution)/shard_map/chain/pallas_call | solution.py:137
  104.5 4.4 %collective-permute-done.13.refs_3_ = f32[20,64,128]{2,1,0:T(8,128)S(1)} collective-permute-done((f32[20,64,128]{2,1,0:T(8,128)S(1)}, f32[20,64,128]{2,1,0:T(8,128)S(1)}, u32[]{:S(2)}, u32[]{:S(2)}) %collective-permute-start.13) | collective-permute-done | bytes 655392 | tf_op jit(solution)/shard_map/ppermute | solution.py:243
  108.9 0.0 collective-permute-done.11.refs_1_
  108.9 2.5 %collective-permute-start.14 = (f32[20,64,128]{2,1,0:T(8,128)S(1)}, f32[20,64,128]{2,1,0:T(8,128)}, u32[]{:S(2)}, u32[]{:S(2)}) collective-permute-start(f32[20,64,128]{2,1,0:T(8,128)S(1)} %constant_dynamic-update-slice_fusion.refs_0_), channel_id=1, source_target_pairs={{0,1},{1,0},{2,3},{3,2},{4,5},{5,4},{6,7},{7,6},{8,9},{9,8},{10,11... | collective-permute-start | bytes 1966088 | tf_op jit(solution)/shard_map/ppermute | solution.py:243
  111.4 0.5 collective-permute-start.16
  111.9 0.0 collective-permute-start.17
  111.9 22.9 %chain.5 = (f32[512,512]{1,0:T(8,128)}, f32[3,512,128]{2,1,0:T(8,128)}, f32[3,128,128]{2,1,0:T(8,128)}) custom-call(f32[8,64,128]{2,1,0:T(8,128)} %copy-done.1, f32[8,64,128]{2,1,0:T(8,128)} %collective-permute-done.1.refs_1_, f32[8,64,128]{2,1,0:T(8,128)} %collective-permute-done.2.refs_2_, f32[8,64,128]{2,1,0:T(8,128)} %copy-done.5, ...), custom_call_target="tpu_custom_call" | custom-call | flops 17999998976 | bytes 48000000 | tf_op jit(solution)/shard_map/chain/pallas_call | solution.py:137
  134.8 0.0 all-gather.3.cloned.1.call-done
  134.9 21.7 %tile.1 = f32[2560,1280]{1,0:T(8,128)} custom-call(s32[2]{0:T(128)} %pad_add_fusion.place_ref, f32[20,64,128]{2,1,0:T(8,128)} %copy-done.2, f32[20,64,128]{2,1,0:T(8,128)} %collective-permute-done.11.refs_1_, f32[20,64,128]{2,1,0:T(8,128)} %collective-permute-done.12.refs_2_, f32[20,64,128]{2,1,0:T(8,128)} %copy-done.4, ...), custom_call_target="tpu_custom_call" | custom-call | flops 12000000000 | bytes 24000000 | tf_op jit(solution)/shard_map/tile/pallas_call | solution.py:226
  (43 shorter events, 0.3 us)
Async XLA Ops:
  6.5 2.7 %copy-start = (bf16[256,4096]{1,0:T(8,128)(2,1)S(1)}, bf16[256,4096]{1,0:T(8,128)(2,1)}, u32[]{:S(2)}) copy-start(bf16[256,4096]{1,0:T(8,128)(2,1)} %param.6) | copy-start | bytes 6291460
  6.5 2.9 %copy-start.3 = (bf16[4096,160]{0,1:T(8,128)(2,1)S(1)}, bf16[4096,160]{0,1:T(8,128)(2,1)}, u32[]{:S(2)}) copy-start(bf16[4096,160]{0,1:T(8,128)(2,1)} %param.8) | copy-start | bytes 3932164
  6.5 128.3 %all-gather.3.cloned.1.call-start = ((), (), s32[]{:S(2)}) async-start(), calls=%async_computation.1 | async-start | bytes 2949120 | tf_op jit(solution)/shard_map/all_gather | solution.py:291
  26.0 5.7 %collective-permute-start = (f32[8,32,128]{2,1,0:T(8,128)S(1)}, f32[8,32,128]{2,1,0:T(8,128)S(1)}, u32[]{:S(2)}, u32[]{:S(2)}) collective-permute-start(f32[8,32,128]{2,1,0:T(8,128)S(1)} %bitcast.42), channel_id=1, source_target_pairs={{0,8},{1,9},{2,10},{3,11},{4,12},{5,13},{6,14},{7,15},{8,0},{9,1},... | collective-permute-start | bytes 393224 | tf_op jit(solution)/shard_map/ppermute | solution.py:243
  31.8 25.6 %copy-start.1 = (f32[8,64,128]{2,1,0:T(8,128)}, f32[8,64,128]{2,1,0:T(8,128)S(1)}, u32[]{:S(2)}) copy-start(f32[8,64,128]{2,1,0:T(8,128)S(1)} %pad_maximum_fusion.2.refs_0_) | copy-start | bytes 786436
  31.8 14.0 %collective-permute-start.3 = (f32[8,64,128]{2,1,0:T(8,128)S(1)}, f32[8,64,128]{2,1,0:T(8,128)S(1)}, u32[]{:S(2)}, u32[]{:S(2)}) collective-permute-start(f32[8,64,128]{2,1,0:T(8,128)S(1)} %pad_maximum_fusion.2.refs_0_), channel_id=1, source_target_pairs={{0,6},{1,7},{2,4},{3,5},{4,2},{5,3},{6,0},{7,1},{8,14},{9,15},{10,... | collective-permute-start | bytes 786440 | tf_op jit(solution)/shard_map/ppermute | solution.py:243
  34.6 12.5 %collective-permute-start.2 = (f32[8,64,128]{2,1,0:T(8,128)S(1)}, f32[8,64,128]{2,1,0:T(8,128)}, u32[]{:S(2)}, u32[]{:S(2)}) collective-permute-start(f32[8,64,128]{2,1,0:T(8,128)S(1)} %pad_maximum_fusion.2.refs_0_), channel_id=1, source_target_pairs={{0,4},{1,5},{2,6},{3,7},{4,0},{5,1},{6,2},{7,3},{8,12},{9,13},{10,... | collective-permute-start | bytes 786440 | tf_op jit(solution)/shard_map/ppermute | solution.py:243
  35.0 12.8 %collective-permute-start.1 = (f32[8,64,128]{2,1,0:T(8,128)S(1)}, f32[8,64,128]{2,1,0:T(8,128)}, u32[]{:S(2)}, u32[]{:S(2)}) collective-permute-start(f32[8,64,128]{2,1,0:T(8,128)S(1)} %pad_maximum_fusion.2.refs_0_), channel_id=1, source_target_pairs={{0,2},{1,3},{2,0},{3,1},{4,6},{5,7},{6,4},{7,5},{8,10},{9,11},{10,... | collective-permute-start | bytes 786440 | tf_op jit(solution)/shard_map/ppermute | solution.py:243
  35.4 13.3 %collective-permute-start.4 = (f32[8,64,128]{2,1,0:T(8,128)S(1)}, f32[8,64,128]{2,1,0:T(8,128)S(1)}, u32[]{:S(2)}, u32[]{:S(2)}) collective-permute-start(f32[8,64,128]{2,1,0:T(8,128)S(1)} %pad_maximum_fusion.2.refs_0_), channel_id=1, source_target_pairs={{0,1},{1,0},{2,3},{3,2},{4,5},{5,4},{6,7},{7,6},{8,9},{9,8},{10,11... | collective-permute-start | bytes 786440 | tf_op jit(solution)/shard_map/ppermute | solution.py:243
  45.8 11.6 %copy-start.5 = (f32[8,64,128]{2,1,0:T(8,128)}, f32[8,64,128]{2,1,0:T(8,128)S(1)}, u32[]{:S(2)}) copy-start(f32[8,64,128]{2,1,0:T(8,128)S(1)} %collective-permute-done.3.refs_3_) | copy-start | bytes 786436
  45.8 8.1 %collective-permute-start.7 = (f32[8,64,128]{2,1,0:T(8,128)S(1)}, f32[8,64,128]{2,1,0:T(8,128)S(1)}, u32[]{:S(2)}, u32[]{:S(2)}) collective-permute-start(f32[8,64,128]{2,1,0:T(8,128)S(1)} %collective-permute-done.3.refs_3_), channel_id=1, source_target_pairs={{0,1},{1,0},{2,3},{3,2},{4,5},{5,4},{6,7},{7,6},{8,9},{9,8},{10,11... | collective-permute-start | bytes 786440 | tf_op jit(solution)/shard_map/ppermute | solution.py:243
  47.1 10.4 %collective-permute-start.6 = (f32[8,64,128]{2,1,0:T(8,128)}, f32[8,64,128]{2,1,0:T(8,128)}, u32[]{:S(2)}, u32[]{:S(2)}) collective-permute-start(f32[8,64,128]{2,1,0:T(8,128)} %collective-permute-done.2.refs_2_), channel_id=1, source_target_pairs={{0,1},{1,0},{2,3},{3,2},{4,5},{5,4},{6,7},{7,6},{8,9},{9,8},{10,11... | collective-permute-start | bytes 786440 | tf_op jit(solution)/shard_map/ppermute | solution.py:243
  47.8 9.6 %collective-permute-start.5 = (f32[8,64,128]{2,1,0:T(8,128)}, f32[8,64,128]{2,1,0:T(8,128)}, u32[]{:S(2)}, u32[]{:S(2)}) collective-permute-start(f32[8,64,128]{2,1,0:T(8,128)} %collective-permute-done.1.refs_1_), channel_id=1, source_target_pairs={{0,1},{1,0},{2,3},{3,2},{4,5},{5,4},{6,7},{7,6},{8,9},{9,8},{10,11... | collective-permute-start | bytes 786440 | tf_op jit(solution)/shard_map/ppermute | solution.py:243
  48.5 24.4 %collective-permute-start.9 = (f32[10,32,128]{2,1,0:T(8,128)S(1)}, f32[10,32,128]{2,1,0:T(8,128)S(1)}, u32[]{:S(2)}, u32[]{:S(2)}) collective-permute-start(f32[10,32,128]{2,1,0:T(8,128)S(1)} %get-tuple-element.43), channel_id=1, source_target_pairs={{0,8},{1,0},{2,24},{3,16},{4,40},{5,32},{6,56},{7,48},{8,72},{9,64... | collective-permute-start | bytes 491528 | tf_op jit(solution)/shard_map/ppermute | solution.py:243
  48.6 5.3 %copy-start.6 = (f32[8,64,128]{2,1,0:T(8,128)}, f32[8,64,128]{2,1,0:T(8,128)S(1)}, u32[]{:S(2)}) copy-start(f32[8,64,128]{2,1,0:T(8,128)S(1)} %collective-permute-done.4.refs_4_) | copy-start | bytes 786436
  48.6 24.3 %collective-permute-start.8 = (f32[10,32,128]{2,1,0:T(8,128)S(1)}, f32[10,32,128]{2,1,0:T(8,128)S(1)}, u32[]{:S(2)}, u32[]{:S(2)}) collective-permute-start(f32[10,32,128]{2,1,0:T(8,128)S(1)} %get-tuple-element.44), channel_id=1, source_target_pairs={{0,0},{1,8},{2,16},{3,24},{4,32},{5,40},{6,48},{7,56},{8,64},{9,72... | collective-permute-start | bytes 491528 | tf_op jit(solution)/shard_map/ppermute | solution.py:243
  54.0 0.7 copy-start.7
  54.7 18.3 %collective-permute-start.10 = (f32[20,32,128]{2,1,0:T(8,128)S(1)}, f32[20,32,128]{2,1,0:T(8,128)S(1)}, u32[]{:S(2)}, u32[]{:S(2)}) collective-permute-start(f32[20,32,128]{2,1,0:T(8,128)S(1)} %bitcast.35), channel_id=1, source_target_pairs={{0,8},{1,9},{2,10},{3,11},{4,12},{5,13},{6,14},{7,15},{8,0},{9,1},... | collective-permute-start | bytes 983048 | tf_op jit(solution)/shard_map/ppermute | solution.py:243
  57.4 17.1 %copy-start.8 = (s32[16]{0:T(128)S(1)}, s32[16]{0:T(128)}, u32[]{:S(2)}) copy-start(s32[16]{0:T(128)} %constant.54.clone) | copy-start | bytes 196
  76.3 32.6 %copy-start.2 = (f32[20,64,128]{2,1,0:T(8,128)}, f32[20,64,128]{2,1,0:T(8,128)S(1)}, u32[]{:S(2)}) copy-start(f32[20,64,128]{2,1,0:T(8,128)S(1)} %constant_dynamic-update-slice_fusion.refs_0_) | copy-start | bytes 1966084
  76.3 32.6 %collective-permute-start.13 = (f32[20,64,128]{2,1,0:T(8,128)S(1)}, f32[20,64,128]{2,1,0:T(8,128)S(1)}, u32[]{:S(2)}, u32[]{:S(2)}) collective-permute-start(f32[20,64,128]{2,1,0:T(8,128)S(1)} %constant_dynamic-update-slice_fusion.refs_0_), channel_id=1, source_target_pairs={{0,6},{1,7},{2,4},{3,5},{4,2},{5,3},{6,0},{7,1},{8,14},{9,15},{10,... | collective-permute-start | bytes 1966088 | tf_op jit(solution)/shard_map/ppermute | solution.py:243
  80.8 28.0 %collective-permute-start.12 = (f32[20,64,128]{2,1,0:T(8,128)S(1)}, f32[20,64,128]{2,1,0:T(8,128)}, u32[]{:S(2)}, u32[]{:S(2)}) collective-permute-start(f32[20,64,128]{2,1,0:T(8,128)S(1)} %constant_dynamic-update-slice_fusion.refs_0_), channel_id=1, source_target_pairs={{0,4},{1,5},{2,6},{3,7},{4,0},{5,1},{6,2},{7,3},{8,12},{9,13},{10,... | collective-permute-start | bytes 1966088 | tf_op jit(solution)/shard_map/ppermute | solution.py:243
  81.4 27.5 %collective-permute-start.11 = (f32[20,64,128]{2,1,0:T(8,128)S(1)}, f32[20,64,128]{2,1,0:T(8,128)}, u32[]{:S(2)}, u32[]{:S(2)}) collective-permute-start(f32[20,64,128]{2,1,0:T(8,128)S(1)} %constant_dynamic-update-slice_fusion.refs_0_), channel_id=1, source_target_pairs={{0,2},{1,3},{2,0},{3,1},{4,6},{5,7},{6,4},{7,5},{8,10},{9,11},{10,... | collective-permute-start | bytes 1966088 | tf_op jit(solution)/shard_map/ppermute | solution.py:243
  108.8 25.9 %copy-start.4 = (f32[20,64,128]{2,1,0:T(8,128)}, f32[20,64,128]{2,1,0:T(8,128)S(1)}, u32[]{:S(2)}) copy-start(f32[20,64,128]{2,1,0:T(8,128)S(1)} %collective-permute-done.13.refs_3_) | copy-start | bytes 1966084
  108.9 25.9 %collective-permute-start.14 = (f32[20,64,128]{2,1,0:T(8,128)S(1)}, f32[20,64,128]{2,1,0:T(8,128)}, u32[]{:S(2)}, u32[]{:S(2)}) collective-permute-start(f32[20,64,128]{2,1,0:T(8,128)S(1)} %constant_dynamic-update-slice_fusion.refs_0_), channel_id=1, source_target_pairs={{0,1},{1,0},{2,3},{3,2},{4,5},{5,4},{6,7},{7,6},{8,9},{9,8},{10,11... | collective-permute-start | bytes 1966088 | tf_op jit(solution)/shard_map/ppermute | solution.py:243
  111.4 23.4 %collective-permute-start.15 = (f32[20,64,128]{2,1,0:T(8,128)}, f32[20,64,128]{2,1,0:T(8,128)}, u32[]{:S(2)}, u32[]{:S(2)}) collective-permute-start(f32[20,64,128]{2,1,0:T(8,128)} %collective-permute-done.11.refs_1_), channel_id=1, source_target_pairs={{0,1},{1,0},{2,3},{3,2},{4,5},{5,4},{6,7},{7,6},{8,9},{9,8},{10,11... | collective-permute-start | bytes 1966088 | tf_op jit(solution)/shard_map/ppermute | solution.py:243
  111.4 23.4 %collective-permute-start.16 = (f32[20,64,128]{2,1,0:T(8,128)}, f32[20,64,128]{2,1,0:T(8,128)}, u32[]{:S(2)}, u32[]{:S(2)}) collective-permute-start(f32[20,64,128]{2,1,0:T(8,128)} %collective-permute-done.12.refs_2_), channel_id=1, source_target_pairs={{0,1},{1,0},{2,3},{3,2},{4,5},{5,4},{6,7},{7,6},{8,9},{9,8},{10,11... | collective-permute-start | bytes 1966088 | tf_op jit(solution)/shard_map/ppermute | solution.py:243
  111.9 23.0 %collective-permute-start.17 = (f32[20,64,128]{2,1,0:T(8,128)S(1)}, f32[20,64,128]{2,1,0:T(8,128)}, u32[]{:S(2)}, u32[]{:S(2)}) collective-permute-start(f32[20,64,128]{2,1,0:T(8,128)S(1)} %collective-permute-done.13.refs_3_), channel_id=1, source_target_pairs={{0,1},{1,0},{2,3},{3,2},{4,5},{5,4},{6,7},{7,6},{8,9},{9,8},{10,11... | collective-permute-start | bytes 1966088 | tf_op jit(solution)/shard_map/ppermute | solution.py:243
Sparse Core Ops, SparseCore 0:
  73.9 39.0 all-gather.2
